TPU v7x, 512 devices: a whole 4x8x8 slice. The times are simulated.
512 devices in a mesh: dp: 32 (over z, x_hi, core), mp: 16 (over y, x_lo).
Axes of the slice: x: 4 (x_hi: 2, x_lo: 2; x = x_hi * 2 + x_lo), y: 8, z: 8, core: 2. Of those that a mesh axis runs over, the one named last changes fastest.
Arguments:
- points: bfloat16 [65536, 1024], P('dp', 'mp'), may hold values from -40 to 40
- point_cluster: int32 [65536, 1], P('dp'), may hold values from 0 to 12287, as said below
- cluster_parent: int32 [12288, 1], P(('dp', 'mp')), may hold values from 0 to 2047, as said below
Outputs:
- level2_centroids: bfloat16 [12288, 1024], P(('dp', 'mp'))
- level3_centroids: bfloat16 [2048, 1024], P('mp')
Inputs may be any that keep to these rules, and one draw needn't show every extreme that they name: `point_cluster`: every level-2 centroid is named by at least one point; split the level-2 centroids into 512 aligned blocks of 24 consecutive ones: the 2048 points of one dp index name centroids of each block exactly 2048 / 512 times. `cluster_parent`: every level-3 centroid is named by at least one level-2 centroid.
All inputs are finite; a program needn't handle non-finite values.
Results may differ from a plain program's by a relative error of at most 0.0048.
Values may be sent and summed in bfloat16 or wider, within the bound.
No kernel may reach another device: no remote copies, remote signals or barrier semaphores. Data moves between devices by JAX's collectives and lax.ppermute only.
A program may use at most 64 MiB of HBM per device.

v0:
```python
import jax
import jax.numpy as jnp
from jax import lax
from jax.sharding import PartitionSpec as P

K2_MP = 768
K3_MP = 128


EPS = 1e-06


def unit_rows(total):
    return total * lax.rsqrt(jnp.mean(total * total, axis=1, keepdims=True) + EPS)


def contract_rows(left, right):
    return lax.dot_general(
        left, right, (((0,), (0,)), ((), ())), preferred_element_type=jnp.float32
    )


def body(points, point_cluster, cluster_parent):
    n_model = lax.axis_size("mp")
    n_data = lax.axis_size("dp")
    model_index = lax.axis_index("mp")
    labels = point_cluster[:, 0]
    rows = K2_MP // n_data
    mine = labels // rows % n_model == model_index
    slot = labels // (n_model * rows) * rows + labels % rows
    slot = jnp.where(mine, slot, -1)
    onehot = (slot[:, None] == lax.iota(jnp.int32, K2_MP)[None, :]).astype(jnp.bfloat16)
    full_rows = lax.all_gather(points, "mp", axis=1, tiled=True)
    sums = lax.psum_scatter(contract_rows(onehot, full_rows), "dp", scatter_dimension=0, tiled=True)
    tally = jnp.sum(onehot, axis=0, dtype=jnp.float32)
    counts = lax.psum_scatter(tally, "dp", scatter_dimension=0, tiled=True)
    level2 = unit_rows(sums).astype(jnp.bfloat16)
    group_c2, group_counts, group_parent = (
        lax.all_gather(level2, "mp", axis=0, tiled=True),
        lax.all_gather(counts.astype(jnp.bfloat16), "mp", axis=0, tiled=True).astype(counts.dtype),
        lax.all_gather(cluster_parent, "mp", axis=0, tiled=True),
    )
    owned = model_index * K3_MP + lax.iota(jnp.int32, K3_MP)
    selector = (group_parent[:, 0][:, None] == owned[None, :]).astype(jnp.float32)
    weighted = group_counts[:, None] * group_c2.astype(jnp.float32)
    partial_parents = lax.dot_general(
        selector,
        weighted,
        (((0,), (0,)), ((), ())),
        precision=lax.Precision.HIGHEST,
        preferred_element_type=jnp.float32,
    )
    parents = lax.psum(partial_parents, "dp")
    level3 = unit_rows(parents).astype(jnp.bfloat16)
    return (level2, level3)


def solution(mesh):
    placed = (P("dp", "mp"), P("dp", None), P(("dp", "mp"), None))
    return jax.shard_map(
        body,
        mesh=mesh,
        in_specs=placed,
        out_specs=(P(("dp", "mp"), None), P("mp", None)),
        check_vma=False,
    )
```

profile of v0, /device:TPU:1, one launch (start us, length us, event | category | flops | bytes accessed | tf_op | source)
XLA Modules:
  0.0 578.5 jit_solution(37435147679488251)
XLA Ops:
  7.2 0.0 all-gather.2.cloned.1.call-start
  7.2 0.7 all-gather.2.cloned.1.call-update
  7.9 0.0 reduce-scatter.2.cloned.1.call-start
  7.9 0.8 compare_select_fusion.2
  8.8 107.5 %all-gather.2.cloned.1.call-done = bf16[2048,1024]{0,1:T(8,128)(2,1)} async-done(((bf16[2048,64]{0,1:T(8,128)(2,1)}), bf16[2048,1024]{0,1:T(8,128)(2,1)}) %all-gather.2.cloned.1.call-update) | async-done | bytes 4194320 | tf_op jit(solution)/shard_map/all_gather | solution.py:33
  116.2 7.7 %fusion.1 = f32[768,1024]{1,0:T(8,128)} fusion(bf16[2048,1024]{0,1:T(8,128)(2,1)} %all-gather.2.cloned.1.call-done, s32[2048]{0:T(1024)S(1)} %bitcast.6), kind=kOutput, calls=%fused_computation.3 | convolution fusion | flops 3224371200 | bytes 7348224 | tf_op jit(solution)/shard_map/dot_general | solution.py:18
  123.9 0.0 copy-start.1
  123.9 0.0 reduce-scatter.2.cloned.1.call-update
  124.0 0.0 all-reduce.5.cloned.1.call-start
  124.0 1.3 dynamic-slice.2
  125.9 0.8 convert_reduce_fusion
  126.7 67.1 %all-reduce.2 = bf16[768]{0:T(1024)(128)(2,1)S(1)} all-reduce(f32[768]{0:T(1024)S(1)} %convert_reduce_fusion), channel_id=3, replica_groups=mesh['dp'=32,'mp'=16] {'dp'}, use_global_device_ids=true, to_apply=%region_3.4.clone | all-reduce | flops 768 | bytes 4608
  193.9 0.1 dynamic-slice.5
  193.9 1.3 dynamic-slice
  195.9 0.2 dynamic-update-slice.1
  196.1 25.2 %all-reduce.1 = bf16[384]{0:T(512)(128)(2,1)S(1)} all-reduce(bf16[384]{0:T(512)(128)(2,1)S(1)} %dynamic-update-slice.1), channel_id=1, replica_groups=mesh['dp'=32,'mp'=16] {'mp'}, use_global_device_ids=true, to_apply=%add.1 | all-reduce | flops 384 | bytes 1536
  221.3 0.0 copy-done.1
  221.3 0.1 bitcast_dynamic-update-slice_fusion
  221.4 9.6 %all-reduce = s32[384]{0:T(512)S(1)} all-reduce(s32[384]{0:T(512)S(1)} %bitcast_dynamic-update-slice_fusion), channel_id=1, replica_groups=mesh['dp'=32,'mp'=16] {'mp'}, use_global_device_ids=true, to_apply=%add | all-reduce | flops 384 | bytes 3072
  231.0 22.3 %reduce-scatter.2.cloned.1.call-done = f32[24,1024]{1,0:T(8,128)} async-done(((f32[768,1024]{1,0:T(8,128)}), f32[24,1024]{1,0:T(8,128)}) %reduce-scatter.2.cloned.1.call-update) | async-done | bytes 98320 | tf_op jit(solution)/shard_map/reduce_scatter | solution.py:34
  253.3 1.0 multiply_reduce_fusion.1
  254.3 1.0 multiply_convert_fusion.1
  255.3 0.0 copy-start
  255.3 30.1 %all_gather.15 = bf16[384,1024]{1,0:T(8,128)(2,1)S(1)} all-gather(bf16[24,1024]{1,0:T(8,128)(2,1)S(1)} %multiply_convert_fusion.1), channel_id=1, replica_groups=mesh['dp'=32,'mp'=16] {'mp'}, dimensions={0}, use_global_device_ids=true | all-gather | bytes 835584 | tf_op jit(solution)/shard_map/all_gather | solution.py:39
  285.5 1.8 fusion.4
  287.2 0.0 all-reduce.5.cloned.1.call-update
  287.3 281.7 %all-reduce.5.cloned.1.call-done = f32[128,1024]{1,0:T(8,128)} async-done(((f32[128,1024]{1,0:T(8,128)}), f32[128,1024]{1,0:T(8,128)}) %all-reduce.5.cloned.1.call-update) | async-done | bytes 524304 | tf_op jit(solution)/shard_map/psum | solution.py:53
  569.0 1.2 multiply_reduce_fusion
  570.1 1.8 multiply_convert_fusion
  572.0 0.0 copy-done
  (6 shorter events, 0.0 us)
Async XLA Ops:
  7.2 109.1 %all-gather.2.cloned.1.call-start = ((), (), s32[]{:S(2)}) async-start(), calls=%async_computation.1 | async-start | bytes 4456448 | tf_op jit(solution)/shard_map/all_gather | solution.py:33
  7.9 245.4 %reduce-scatter.2.cloned.1.call-start = ((), (), s32[]{:S(2)}) async-start(), calls=%async_computation.2 | async-start | bytes 3244032 | tf_op jit(solution)/shard_map/reduce_scatter | solution.py:34
  123.9 97.4 %copy-start.1 = (s32[24,1]{0,1:T(1,128)S(1)}, s32[24,1]{0,1:T(1,128)}, u32[]{:S(2)}) copy-start(s32[24,1]{0,1:T(1,128)} %param.5) | copy-start | bytes 292
  124.0 445.0 %all-reduce.5.cloned.1.call-start = ((), (), s32[]{:S(2)}) async-start(), calls=%async_computation.3 | async-start | bytes 1048576 | tf_op jit(solution)/shard_map/psum | solution.py:53
  255.3 316.7 %copy-start = (bf16[24,1024]{1,0:T(8,128)(2,1)}, bf16[24,1024]{1,0:T(8,128)(2,1)S(1)}, u32[]{:S(2)}) copy-start(bf16[24,1024]{1,0:T(8,128)(2,1)S(1)} %multiply_convert_fusion.1) | copy-start | bytes 147460
Sparse Core Ops, SparseCore 0:
  10.1 106.1 all-gather.1
  124.1 129.2 reduce-scatter.1
  287.4 281.5 all-reduce.4
where the time goes:
time: 579 us
  waiting for transfers between devices  412 us (71%)
  blocking collectives  132 us (23%)
  between operations  15.1 us (3%)
  matrix products  9.45 us (2%)
  other arithmetic  6.63 us (1%)
    psum x1, waiting for transfers between devices, body(): parents = lax.psum(partial_parents, 'dp')  282 us
    all_gather x1, waiting for transfers between devices, body(): full_rows = lax.all_gather(points, 'mp', axis=1, tiled=True)  107 us
    unnamed x3, blocking collectives  102 us
    all_gather x1, blocking collectives, body(): lax.all_gather(level2, 'mp', axis=0, tiled=True)  30.1 us
    reduce_scatter x1, waiting for transfers between devices, body(): lax.psum_scatter(contract_rows(onehot, full_rows), 'dp', scatter_dimensio...  22.3 us
  transfers between devices with their start and end apart: 3, of which 3 were waited for; matrix products, arithmetic and copies ran while one was open for 1% of the time, Pallas kernels for 0%

commit v1 on v0

v1 whole, which is shorter than its diff:
```python
import jax
import jax.numpy as jnp
from jax import lax
from jax.experimental import pallas as pl
from jax.experimental.pallas import tpu as pltpu
from jax.sharding import PartitionSpec as P

N_DP = 32
N_MP = 16
PTS = 2048
FEAT = 64
ROWS = 24
GROUP = ROWS * N_MP
D = 1024
K3 = 2048
K3_MP = 128
EPS = 1e-06

f32 = jnp.float32
bf16 = jnp.bfloat16
i32 = jnp.int32


def iota(shape, dim):
    return lax.broadcasted_iota(i32, shape, dim)


def hot(mask):
    return jnp.where(mask, 1.0, 0.0).astype(bf16)


def dot_nt(a, b):
    return lax.dot_general(a, b, (((1,), (1,)), ((), ())), preferred_element_type=f32)


def dot_nn(a, b):
    return lax.dot_general(a, b, (((1,), (0,)), ((), ())), preferred_element_type=f32)


def sort_kernel(labels_ref, points_ref, out_ref):
    labels = labels_ref[...]
    group = ((labels >> 7) * 171) >> 9
    local = labels - group * GROUP
    member = jnp.where(iota((N_DP, PTS), 0) == group, 1.0, 0.0)
    member16 = member.astype(bf16)
    width = 256
    n_chunks = PTS // width
    stacked = jnp.concatenate(
        [member16[:, c * width : (c + 1) * width] for c in range(n_chunks)], axis=0
    )
    before = hot(iota((width, 2 * width), 0) < iota((width, 2 * width), 1))
    prefix = dot_nn(stacked, before)
    base = jnp.zeros((N_DP, width), f32)
    ranks = []
    for c in range(n_chunks):
        part = prefix[c * N_DP : (c + 1) * N_DP]
        inside = member[:, c * width : (c + 1) * width]
        ranks.append(jnp.sum(inside * (part[:, :width] + base), axis=0, keepdims=True))
        base = base + part[:, width:]
    rank = jnp.concatenate(ranks, axis=1).astype(i32)
    r1 = rank & 3
    r2 = rank >> 2

    points = points_ref[...]
    split = jnp.concatenate([points * hot(r1 == r) for r in range(4)], axis=0)
    key = hot(iota((N_DP * 16, PTS), 0) == group * 16 + r2)
    moved = dot_nt(key, split)
    out_ref[:, 0:16, :] = moved[:, :128].reshape(N_DP, 16, 128).astype(bf16)
    out_ref[:, 16:32, :] = moved[:, 128:].reshape(N_DP, 16, 128).astype(bf16)

    side = r1 & 1
    high = (local >> 3).astype(f32)
    low = (local & 7).astype(f32)
    zero = jnp.zeros((4, PTS), f32)
    parts = jnp.concatenate(
        [
            jnp.where(side == 0, high, 0.0),
            jnp.where(side == 1, high, 0.0),
            jnp.where(side == 0, low, 0.0),
            jnp.where(side == 1, low, 0.0),
            zero,
        ],
        axis=0,
    )
    tagged = jnp.where(
        iota((N_DP, 8, PTS), 0) == group.reshape(1, 1, PTS), parts.reshape(1, 8, PTS), 0.0
    )
    place = hot(iota((128, PTS), 0) == (r1 >> 1) * 16 + r2)
    tags = dot_nt(tagged.reshape(N_DP * 8, PTS).astype(bf16), place)
    out_ref[:, 32:40, :] = tags.reshape(N_DP, 8, 128).astype(bf16)


def sum_kernel(in_ref, out_ref):
    data = in_ref[:, 0:32, :].reshape(N_DP * 32, 128)
    tags = in_ref[:, 32:40, :].astype(f32)
    sides = ([], [])
    for n in range(8):
        tile = tags[4 * n]
        for q in range(1, 4):
            tile = tile + pltpu.roll(tags[4 * n + q], 32 * q, 1)
        for s in range(2):
            sides[s].append(8.0 * tile[s : s + 1] + tile[2 + s : 3 + s])
    data = jnp.concatenate([data, jnp.ones((N_DP * 32, 128), bf16)], axis=1)
    totals = []
    for s in range(2):
        label = jnp.concatenate(sides[s], axis=1).astype(i32)
        totals.append(dot_nn(hot(iota((GROUP, N_DP * 32), 0) == label), data))
    lane = iota((GROUP, 128), 1)
    sums = jnp.where(lane < 64, totals[0][:, :128], totals[1][:, :128])
    sums = (sums + pltpu.roll(sums, 64, 1)).reshape(N_MP, 3, 8, 128)
    counts = (totals[0][:, 128:] + totals[1][:, 128:]).reshape(N_MP, 3, 8, 128)
    lane = iota((N_MP, 8, 128), 2)
    out_ref[:, 0:8, :] = jnp.where(lane < 64, sums[:, 0], sums[:, 1])
    tail = jnp.where(lane < 80, counts[:, 0], jnp.where(lane < 96, counts[:, 1], counts[:, 2]))
    out_ref[:, 8:16, :] = jnp.where(lane < 64, sums[:, 2], tail)


def unit_kernel(in_ref, parent_ref, level2_ref, out_ref):
    lane = iota((8, 128), 1)
    left = lane < 64
    rows = ([], [], [])
    for c in range(N_MP // 2):
        even, odd = in_ref[2 * c], in_ref[2 * c + 1]
        rows[0].append(jnp.where(left, even[:8], pltpu.roll(odd[:8], 64, 1)))
        rows[1].append(jnp.where(left, pltpu.roll(even[:8], 64, 1), odd[:8]))
        rows[2].append(jnp.where(left, even[8:], pltpu.roll(odd[8:], 64, 1)))
    tail = in_ref[0][8:]
    parent = parent_ref[...].astype(f32)
    level2 = []
    meta = jnp.zeros((8, 128), f32)
    for g in range(3):
        square = rows[g][0] * rows[g][0]
        for c in range(1, N_MP // 2):
            square = square + rows[g][c] * rows[g][c]
        scale = lax.rsqrt(jnp.sum(square, axis=1, keepdims=True) * (1.0 / D) + EPS)
        level2.append([(r * scale).astype(bf16).astype(f32) for r in rows[g]])
        pick = iota((8, ROWS), 1) == iota((8, ROWS), 0) + 8 * g
        mine = jnp.sum(jnp.where(pick, parent, 0.0), axis=1, keepdims=True).astype(i32)
        meta = jnp.where(lane == 96 + 4 * g, tail[:, 64 + 16 * g : 65 + 16 * g], meta)
        meta = jnp.where(lane == 97 + 4 * g, (mine >> 3).astype(f32), meta)
        meta = jnp.where(lane == 98 + 4 * g, (mine & 7).astype(f32), meta)
    level2_ref[...] = jnp.concatenate(
        [jnp.concatenate(level2[g], axis=1) for g in range(3)], axis=0
    ).astype(bf16)
    pieces = []
    for i in range(N_DP):
        c, b = divmod(i, 4)
        piece = meta
        for g in range(3):
            turned = level2[g][c]
            if g != b:
                turned = pltpu.roll(turned, (32 * (g - b)) % 128, 1)
            piece = jnp.where((lane >= 32 * g) & (lane < 32 * (g + 1)), turned, piece)
        pieces.append(piece.reshape(1, 8, 128))
    out_ref[...] = jnp.concatenate(pieces, axis=0).astype(bf16)


def parent_kernel(in_ref, out_ref):
    rows = N_DP * 8
    x = in_ref[...].astype(f32).reshape(rows, 128)
    lane = iota((rows, 128), 1)
    count = jnp.zeros((rows, 128), f32)
    for g in range(3):
        inside = (lane >= 32 * g) & (lane < 32 * (g + 1))
        count = jnp.where(inside, x[:, 96 + 4 * g : 97 + 4 * g], count)
    weighted = x * count
    high = weighted.astype(bf16).astype(f32)
    low = weighted - high
    high, low = high.T.astype(bf16), low.T.astype(bf16)
    total = jnp.zeros((64, K3), f32)
    for g in range(3):
        parent = (8.0 * x[:, 97 + 4 * g : 98 + 4 * g] + x[:, 98 + 4 * g : 99 + 4 * g]).astype(i32)
        chosen = hot(iota((rows, K3), 1) == parent)
        both = jnp.concatenate([high[32 * g : 32 * g + 32], low[32 * g : 32 * g + 32]], axis=0)
        total = total + dot_nn(both, chosen)
    total = total[:32] + total[32:]
    for j in range(N_MP):
        out_ref[j] = total[:, K3_MP * j : K3_MP * (j + 1)]


def spread_kernel(in_ref, out_ref):
    total = jnp.sum(in_ref[...], axis=0).astype(bf16)
    out_ref[...] = jnp.broadcast_to(total[None], (N_DP, 32, 128))


def finish_kernel(in_ref, out_ref):
    x = in_ref[...].astype(f32).reshape(D, 128)
    scale = lax.rsqrt(jnp.sum(x * x, axis=0, keepdims=True) * (1.0 / D) + EPS)
    y = x * scale
    for c in range(8):
        out_ref[:, 128 * c : 128 * (c + 1)] = y[128 * c : 128 * (c + 1)].T.astype(bf16)


def call(kernel, out, *args):
    vmem = pl.BlockSpec(memory_space=pltpu.VMEM)
    many = isinstance(out, tuple)
    return pl.pallas_call(
        kernel,
        out_shape=out,
        in_specs=[vmem] * len(args),
        out_specs=(vmem,) * len(out) if many else vmem,
        compiler_params=pltpu.CompilerParams(vmem_limit_bytes=48 * 1024 * 1024),
    )(*args)


def shape(dims, dtype):
    return jax.ShapeDtypeStruct(dims, dtype)


def exchange(x, axis):
    return lax.all_to_all(x, axis, 0, 0, tiled=True)


def body(points, point_cluster, cluster_parent):
    sent = call(sort_kernel, shape((N_DP, 40, 128), bf16), point_cluster.T, points.T)
    sums = call(sum_kernel, shape((N_MP, 16, 128), f32), exchange(sent, "dp"))
    level2, cut = call(
        unit_kernel,
        (shape((ROWS, D), bf16), shape((N_DP, 8, 128), bf16)),
        exchange(sums, "mp"),
        cluster_parent.T,
    )
    partial = call(parent_kernel, shape((N_MP, 32, 128), f32), exchange(cut, "dp"))
    parents = call(spread_kernel, shape((N_DP, 32, 128), bf16), exchange(partial, "mp"))
    level3 = call(finish_kernel, shape((K3_MP, D), bf16), exchange(parents, "dp"))
    return (level2, level3)


def solution(mesh):
    placed = (P("dp", "mp"), P("dp", None), P(("dp", "mp"), None))
    return jax.shard_map(
        body,
        mesh=mesh,
        in_specs=placed,
        out_specs=(P(("dp", "mp"), None), P("mp", None)),
        check_vma=False,
    )
```

time: 579 us -> 99.3 us (0.17)
  waiting for transfers between devices: 412 us -> 0 us
  blocking collectives: 132 us -> 91.3 us
  between operations: 15.1 us -> 0.66 us
  matrix products: 9.45 us -> 0 us
  other arithmetic: 6.63 us -> 0 us
    psum x1 -> x0, waiting for transfers between devices: 282 us -> none  [body(): parents = lax.psum(partial_parents, 'dp')]
    all_gather x1 -> x0, waiting for transfers between devices: 107 us -> none  [body(): full_rows = lax.all_gather(points, 'mp', axis=1, tiled=True)]
    unnamed x3 -> x0, blocking collectives: 102 us -> none
    all_to_all x0 -> x5, blocking collectives: none -> 91.3 us  [exchange(): return lax.all_to_all(x, axis, 0, 0, tiled=True)]
    all_gather x1 -> x0, blocking collectives: 30.1 us -> none  [body(): lax.all_gather(level2, 'mp', axis=0, tiled=True)]
    reduce_scatter x1 -> x0, waiting for transfers between devices: 22.3 us -> none  [body(): lax.psum_scatter(contract_rows(onehot, full_rows), 'dp', scatter_dimensio...]
    dot_general x2 -> x0, matrix products: 9.45 us -> none  [the longest x1 7.69 us: contract_rows(): lax.dot_general(left, right, (((0,), (0,)), ((), ())), preferred_element_...]
  transfers between devices with their start and end apart: 3 -> 0, of which waited for: 3 -> 0; matrix products, arithmetic and copies ran while one was open for 1% -> 0% of each run, Pallas kernels for 0% -> 0%
where the time goes in v1:
time: 99.3 us; the launch traced here: 98.9 us
  blocking collectives  91.3 us (92%)
  Pallas kernels  4.7 us (5%)
  local copies, waits for them, and re-layouts  2.29 us (2%)
    all_to_all x5, blocking collectives, exchange(): return lax.all_to_all(x, axis, 0, 0, tiled=True)  91.3 us
    pallas_call x6, Pallas kernels, call(): pl.pallas_call(kernel, out_shape=out, in_specs=[vmem] * len(args), out_sp...  4.7 us
    unnamed x6, local copies, waits for them, and re-layouts  2.29 us

profile of v1, /device:TPU:1, one launch (start us, length us, event | category | flops | bytes accessed | tf_op | source)
XLA Modules:
  0.0 98.9 jit_solution(11233445839508813277)
XLA Ops:
  0.6 0.0 copy-start
  0.6 0.9 copy-done
  1.6 0.0 copy-start.1
  1.6 0.7 copy-done.1
  2.3 1.3 %shard_map.50 = bf16[32,40,128]{2,1,0:T(8,128)(2,1)S(1)} custom-call(s32[1,2048]{1,0:T(1,128)S(1)} %bitcast.4, bf16[64,2048]{1,0:T(8,128)(2,1)S(1)} %bitcast.3), custom_call_target="tpu_custom_call" | custom-call | tf_op jit(solution)/shard_map/pallas_call | solution.py:197
  3.6 27.5 %all_to_all.25.in_ref = bf16[32,40,128]{2,1,0:T(8,128)(2,1)S(1)} all-to-all(bf16[32,40,128]{2,1,0:T(8,128)(2,1)S(1)} %shard_map.50), channel_id=1, replica_groups=mesh['dp'=32,'mp'=16] {'dp'}, dimensions={0} | all-to-all | bytes 655360 | tf_op jit(solution)/shard_map/all_to_all | solution.py:211
  31.1 0.7 shard_map.51
  31.8 15.3 %all_to_all.26.in_ref = f32[16,16,128]{2,1,0:T(8,128)S(1)} all-to-all(f32[16,16,128]{2,1,0:T(8,128)S(1)} %shard_map.51), channel_id=1, replica_groups=mesh['dp'=32,'mp'=16] {'mp'}, dimensions={0} | all-to-all | bytes 262144 | tf_op jit(solution)/shard_map/all_to_all | solution.py:211
  47.1 0.0 copy-start.2
  47.1 0.7 copy-done.2
  47.7 0.8 shard_map.52
  48.5 16.8 %all_to_all.27.in_ref = bf16[32,8,128]{2,1,0:T(8,128)(2,1)S(1)} all-to-all(bf16[32,8,128]{2,1,0:T(8,128)(2,1)S(1)} %get-tuple-element.5), channel_id=1, replica_groups=mesh['dp'=32,'mp'=16] {'dp'}, dimensions={0} | all-to-all | bytes 131072 | tf_op jit(solution)/shard_map/all_to_all | solution.py:211
  65.4 0.9 shard_map.53
  66.2 13.9 %all_to_all.28.in_ref = f32[16,32,128]{2,1,0:T(8,128)S(1)} all-to-all(f32[16,32,128]{2,1,0:T(8,128)S(1)} %shard_map.53), channel_id=1, replica_groups=mesh['dp'=32,'mp'=16] {'mp'}, dimensions={0} | all-to-all | bytes 524288 | tf_op jit(solution)/shard_map/all_to_all | solution.py:211
  80.2 17.7 %all_to_all.29.in_ref = bf16[32,32,128]{2,1,0:T(8,128)(2,1)S(1)} all-to-all(bf16[32,32,128]{2,1,0:T(8,128)(2,1)S(1)} %shard_map.54), channel_id=1, replica_groups=mesh['dp'=32,'mp'=16] {'dp'}, dimensions={0} | all-to-all | bytes 524288 | tf_op jit(solution)/shard_map/all_to_all | solution.py:211
  97.9 1.0 %shard_map.55 = bf16[128,1024]{1,0:T(8,128)(2,1)} custom-call(bf16[32,32,128]{2,1,0:T(8,128)(2,1)S(1)} %all_to_all.29.in_ref), custom_call_target="tpu_custom_call" | custom-call | tf_op jit(solution)/shard_map/pallas_call | solution.py:197
  (1 shorter events, 0.0 us)
Async XLA Ops:
  0.6 1.0 copy-start
  1.6 0.7 copy-start.1
  47.1 0.7 copy-start.2

commit v2 on v0

v2 whole, which is shorter than its diff:
```python
import jax
import jax.numpy as jnp
from jax import lax
from jax.experimental import pallas as pl
from jax.experimental.pallas import tpu as pltpu
from jax.sharding import PartitionSpec as P

N_DP = 32
N_MP = 16
PTS = 2048
FEAT = 64
ROWS = 24
GROUP = ROWS * N_MP
D = 1024
K3 = 2048
K3_MP = 128
EPS = 1e-06
STRIDE = 34

f32 = jnp.float32
bf16 = jnp.bfloat16
i32 = jnp.int32


def iota(shape, dim):
    return lax.broadcasted_iota(i32, shape, dim)


def hot(mask):
    return jnp.where(mask, 1.0, 0.0).astype(bf16)


def dot_nt(a, b):
    return lax.dot_general(a, b, (((1,), (1,)), ((), ())), preferred_element_type=f32)


def dot_nn(a, b):
    return lax.dot_general(a, b, (((1,), (0,)), ((), ())), preferred_element_type=f32)


def sort_kernel(labels_hbm, points_hbm, out_ref, labels_ref, points_ref, rows_ref, sems):
    fetch_labels = pltpu.make_async_copy(labels_hbm, labels_ref, sems.at[0])
    fetch_points = pltpu.make_async_copy(points_hbm, points_ref, sems.at[1])
    fetch_labels.start()
    fetch_points.start()
    fetch_labels.wait()
    labels = labels_ref[...]
    group = ((labels >> 7) * 171) >> 9
    local = labels - group * GROUP
    member = jnp.where(iota((N_DP, PTS), 0) == group, 1.0, 0.0)
    member16 = member.astype(bf16)
    width = 256
    n_chunks = PTS // width
    stacked = jnp.concatenate(
        [member16[:, c * width : (c + 1) * width] for c in range(n_chunks)], axis=0
    )
    before = hot(iota((width, 2 * width), 0) < iota((width, 2 * width), 1))
    prefix = dot_nn(stacked, before)
    base = jnp.zeros((N_DP, width), f32)
    ranks = []
    for c in range(n_chunks):
        part = prefix[c * N_DP : (c + 1) * N_DP]
        inside = member[:, c * width : (c + 1) * width]
        ranks.append(jnp.sum(inside * (part[:, :width] + base), axis=0, keepdims=True))
        base = base + part[:, width:]
    rank = jnp.concatenate(ranks, axis=1).astype(i32)
    r1 = rank & 3
    r2 = rank >> 2
    key = hot(iota((N_DP * 16, PTS), 0) == group * 16 + r2)

    line = iota((2 * N_DP, PTS), 0)
    digit = jnp.where((line & 1) == 0, local >> 3, local & 7).astype(f32)
    digit = jnp.where((line >> 1) == group, digit, 0.0).astype(bf16)
    turn = lax.axis_index("dp") * STRIDE
    spot = (turn + (r1 >> 1) * 16 + r2 + 64 * (r1 & 1)) & 127
    tags = dot_nt(digit, hot(iota((128, PTS), 0) == spot))

    fetch_points.wait()
    points = points_ref[...]
    split = jnp.concatenate([points * hot(r1 == r) for r in range(4)], axis=0)
    moved = dot_nt(key, split)
    for d in range(N_DP):
        rows_ref[STRIDE * d : STRIDE * d + 16, :] = moved[16 * d : 16 * d + 16, :128]
        rows_ref[STRIDE * d + 16 : STRIDE * d + 32, :] = moved[16 * d : 16 * d + 16, 128:]
        rows_ref[STRIDE * d + 32 : STRIDE * d + 34, :] = tags[2 * d : 2 * d + 2]
    out_ref[...] = rows_ref[...].astype(bf16)


def sum_kernel(parent_hbm, in_ref, out_ref, keep_ref, parent_ref, sem):
    fetch = pltpu.make_async_copy(parent_hbm, parent_ref, sem)
    fetch.start()
    total = N_DP * STRIDE
    data = in_ref[...]
    line, column = iota((N_DP, total), 0) * STRIDE, iota((N_DP, total), 1)
    weight = jnp.where(column == line + 32, 8.0, jnp.where(column == line + 33, 1.0, 0.0))
    tags = dot_nn(weight.astype(bf16), data)
    data = jnp.concatenate([data, jnp.ones((total, 128), bf16)], axis=1)
    results = []
    for s in range(2):
        if s == 1:
            tags = pltpu.roll(tags, 64, 1)
        tiles = []
        for t in range(-(-total // 128)):
            place = iota((N_DP, 128), 1) + 128 * t
            source = (place * 1928) >> 16
            tile = jnp.where(source == iota((N_DP, 128), 0), tags, 0.0)
            tile = jnp.sum(tile, axis=0, keepdims=True)
            tiles.append(jnp.where((place - source * STRIDE)[:1] < 32, tile, -1.0))
        label = jnp.concatenate(tiles, axis=1)[:, :total].astype(i32)
        results.append(dot_nn(hot(iota((GROUP, total), 0) == label), data))
    left = iota((GROUP, 128), 1) < 64
    sums = jnp.where(left, results[0][:, :128], results[1][:, :128])
    sums = sums + pltpu.roll(sums, 64, 1)
    counts = results[0][:, 128:] + results[1][:, 128:]
    turned = jnp.where(left, sums, counts).T
    keep_ref[...] = turned[:72]
    squares = jnp.sum(turned[:64] * turned[:64], axis=0, keepdims=True)
    squares = jnp.concatenate([squares[:, 128 * c : 128 * (c + 1)] for c in range(3)], axis=0)
    sums = sums.reshape(N_MP, 3, 8, 128)
    half = iota((N_MP, 8, 128), 2) < 64
    out_ref[:, 0:8, :] = jnp.where(half, sums[:, 0], sums[:, 1])
    last = sums[:, 2]
    out_ref[:, 8:12, :] = jnp.where(half[:, :4], last[:, :4], last[:, 4:])
    out_ref[:, 12:15, :] = jnp.broadcast_to(squares[None], (N_MP, 3, 128))
    fetch.wait()
    parent = parent_ref[...].astype(f32)
    parent = jnp.concatenate([parent, jnp.zeros((1, 128 - ROWS), f32)], axis=1)
    out_ref[:, 15:16, :] = jnp.broadcast_to(parent[None], (N_MP, 1, 128))


def unit_kernel(in_ref, keep_ref, level2_ref, out_ref):
    left = iota((8, 128), 1) < 64
    rows = ([], [], [])
    for c in range(N_MP // 2):
        even, odd = in_ref[2 * c], in_ref[2 * c + 1]
        turned_even, turned_odd = pltpu.roll(even, 64, 1), pltpu.roll(odd, 64, 1)
        rows[0].append(jnp.where(left, even[:8], turned_odd[:8]))
        rows[1].append(jnp.where(left, turned_even[:8], odd[:8]))
        upper = jnp.where(left, even[8:], turned_odd[8:])[:4]
        lower = jnp.where(left, turned_even[8:], odd[8:])[:4]
        rows[2].append(jnp.concatenate([upper, lower], axis=0))
    lines = jnp.concatenate([jnp.concatenate(r, axis=1) for r in rows], axis=0)
    scale = lax.rsqrt(jnp.sum(lines * lines, axis=1, keepdims=True) * (1.0 / D) + EPS)
    level2_ref[...] = (lines * scale).astype(bf16)

    squares = jnp.sum(in_ref[:, 8:16, :], axis=0)
    squares = jnp.concatenate([squares[4 + c : 5 + c] for c in range(3)], axis=1)
    scale = lax.rsqrt(squares * (1.0 / D) + EPS)
    named = jnp.concatenate(
        [pltpu.roll(in_ref[j, 15:16, :], (ROWS * j) % 128, 1) for j in range(N_MP)], axis=0
    )
    parent = []
    for c in range(3):
        place = iota((N_MP, 128), 1) + 128 * c
        mine = ((place >> 3) * 171) >> 9 == iota((N_MP, 128), 0)
        parent.append(jnp.sum(jnp.where(mine, named, 0.0), axis=0, keepdims=True))
    parent = jnp.concatenate(parent, axis=1).astype(i32)
    side = (parent >> 5) & 1
    device = (parent & 31) * N_MP + (parent >> 7)
    key = hot(iota((2 * N_DP * N_MP, GROUP), 0) == device * 2 + ((parent >> 6) & 1))

    weighted = (keep_ref[0:64, :] * scale).astype(bf16).astype(f32) * keep_ref[64:65, :]
    both = jnp.concatenate(
        [jnp.where(side == 0, weighted, 0.0), jnp.where(side == 1, weighted, 0.0)], axis=0
    )
    high = both.astype(bf16)
    low = (both - high.astype(f32)).astype(bf16)
    out_ref[...] = (dot_nt(key, high) + dot_nt(key, low)).astype(bf16)


def spread_kernel(in_ref, out_ref):
    total = jnp.sum(in_ref[...].astype(f32).reshape(N_DP, 32, 128), axis=0)
    left = iota((32, 128), 1) < 64
    above = pltpu.roll(total, 30, 0)
    first = jnp.where(left, total, pltpu.roll(above, 64, 1))
    second = jnp.where(left, pltpu.roll(total, 64, 1), above)
    rows = jnp.where((iota((32, 128), 0) & 3) < 2, first, pltpu.roll(second, 2, 0))
    square = jnp.sum((rows * rows).reshape(4, 8, 128), axis=0)
    square = jnp.sum(square + pltpu.roll(square, 4, 0), axis=1, keepdims=True)
    scale = lax.rsqrt(square * (1.0 / D) + EPS)
    rows = (rows.reshape(4, 8, 128) * scale[None]).reshape(32, 128)
    out_ref[...] = jnp.broadcast_to(rows.astype(bf16)[None], (N_DP, 32, 128))


def finish_kernel(in_ref, out_ref, rows_ref):
    rows_ref[...] = in_ref[...].astype(f32).reshape(N_DP * 32, 128)
    for c in range(8):
        for q, r in enumerate((0, 2, 1, 3)):
            out_ref[32 * r : 32 * (r + 1), 128 * c : 128 * (c + 1)] = rows_ref[
                pl.ds(4 * c + q, N_DP, stride=32), :
            ].astype(bf16)


def call(kernel, out, *args, far=(), scratch=()):
    vmem = pl.BlockSpec(memory_space=pltpu.VMEM)
    many = isinstance(out, tuple)
    return pl.pallas_call(
        kernel,
        out_shape=out,
        in_specs=[pl.BlockSpec(memory_space=pltpu.HBM)] * len(far) + [vmem] * len(args),
        out_specs=(vmem,) * len(out) if many else vmem,
        scratch_shapes=scratch,
        compiler_params=pltpu.CompilerParams(vmem_limit_bytes=48 * 1024 * 1024),
    )(*(pltpu.with_memory_space_constraint(x, pltpu.HBM) for x in far), *args)


def shape(dims, dtype):
    return jax.ShapeDtypeStruct(dims, dtype)


def exchange(x, axis):
    return lax.all_to_all(x, axis, 0, 0, tiled=True)


def body(points, point_cluster, cluster_parent):
    rows = N_DP * STRIDE
    sent = call(
        sort_kernel,
        shape((rows, 128), bf16),
        far=(point_cluster.T, points.T),
        scratch=(
            pltpu.VMEM((1, PTS), i32),
            pltpu.VMEM((FEAT, PTS), bf16),
            pltpu.VMEM((rows, 128), f32),
            pltpu.SemaphoreType.DMA((2,)),
        ),
    )
    got = exchange(sent.reshape(N_DP, STRIDE // 2, 2, 128), "dp").reshape(rows, 128)
    sums, keep = call(
        sum_kernel,
        (shape((N_MP, 16, 128), f32), shape((72, GROUP), f32)),
        got,
        far=(cluster_parent.T,),
        scratch=(pltpu.VMEM((1, ROWS), i32), pltpu.SemaphoreType.DMA(())),
    )
    devices = N_DP * N_MP
    level2, partial = call(
        unit_kernel,
        (shape((ROWS, D), bf16), shape((2 * devices, 128), bf16)),
        exchange(sums, "mp"),
        keep,
    )
    parts = exchange(partial.reshape(devices, 2, 128), ("dp", "mp")).reshape(2 * devices, 128)
    parents = call(spread_kernel, shape((N_DP, 32, 128), bf16), parts)
    level3 = call(
        finish_kernel,
        shape((K3_MP, D), bf16),
        exchange(parents, "dp"),
        scratch=(pltpu.VMEM((N_DP * 32, 128), f32),),
    )
    return (level2, level3)


def solution(mesh):
    placed = (P("dp", "mp"), P("dp", None), P(("dp", "mp"), None))
    return jax.shard_map(
        body,
        mesh=mesh,
        in_specs=placed,
        out_specs=(P(("dp", "mp"), None), P("mp", None)),
        check_vma=False,
    )
```

time: 579 us -> 95.4 us (0.16)
  waiting for transfers between devices: 412 us -> 0 us
  blocking collectives: 132 us -> 88.1 us
  between operations: 15.1 us -> 0.66 us
  matrix products: 9.45 us -> 0 us
  other arithmetic: 6.63 us -> 0 us
  Pallas kernels: 0 us -> 6.43 us
    psum x1 -> x0, waiting for transfers between devices: 282 us -> none  [body(): parents = lax.psum(partial_parents, 'dp')]
    all_gather x1 -> x0, waiting for transfers between devices: 107 us -> none  [body(): full_rows = lax.all_gather(points, 'mp', axis=1, tiled=True)]
    unnamed x3 -> x0, blocking collectives: 102 us -> none
    all_to_all x0 -> x4, blocking collectives: none -> 88.1 us  [exchange(): return lax.all_to_all(x, axis, 0, 0, tiled=True)]
    all_gather x1 -> x0, blocking collectives: 30.1 us -> none  [body(): lax.all_gather(level2, 'mp', axis=0, tiled=True)]
    reduce_scatter x1 -> x0, waiting for transfers between devices: 22.3 us -> none  [body(): lax.psum_scatter(contract_rows(onehot, full_rows), 'dp', scatter_dimensio...]
    dot_general x2 -> x0, matrix products: 9.45 us -> none  [the longest x1 7.69 us: contract_rows(): lax.dot_general(left, right, (((0,), (0,)), ((), ())), preferred_element_...]
    pallas_call x0 -> x5, Pallas kernels: none -> 6.43 us  [call(): pl.pallas_call(kernel, out_shape=out, in_specs=[pl.BlockSpec(memory_space...]
  transfers between devices with their start and end apart: 3 -> 0, of which waited for: 3 -> 0; matrix products, arithmetic and copies ran while one was open for 1% -> 0% of each run, Pallas kernels for 0% -> 0%
where the time goes in v2:
time: 95.4 us; the launch traced here: 95.2 us
  blocking collectives  88.1 us (92%)
  Pallas kernels  6.43 us (7%)
    all_to_all x4, blocking collectives, exchange(): return lax.all_to_all(x, axis, 0, 0, tiled=True)  88.1 us
    pallas_call x5, Pallas kernels, call(): pl.pallas_call(kernel, out_shape=out, in_specs=[pl.BlockSpec(memory_space...  6.43 us

profile of v2, /device:TPU:1, one launch (start us, length us, event | category | flops | bytes accessed | tf_op | source)
XLA Modules:
  0.0 95.2 jit_solution(2061173354010367738)
XLA Ops:
  0.6 2.8 %shard_map.50 = bf16[1088,128]{1,0:T(8,128)(2,1)S(1)} custom-call(s32[1,2048]{1,0:T(1,128)} %bitcast.12, bf16[64,2048]{1,0:T(8,128)(2,1)} %bitcast.11), custom_call_target="tpu_custom_call" | custom-call | tf_op jit(solution)/shard_map/pallas_call | solution.py:197
  3.4 27.5 %all_to_all.20 = bf16[32,17,2,128]{3,2,1,0:T(2,128)(2,1)S(1)} all-to-all(bf16[32,17,2,128]{3,2,1,0:T(2,128)(2,1)S(1)} %bitcast.8), channel_id=1, replica_groups=mesh['dp'=32,'mp'=16] {'dp'}, dimensions={0} | all-to-all | bytes 557056 | tf_op jit(solution)/shard_map/all_to_all | solution.py:212
  30.9 1.0 %shard_map.51 = (f32[16,16,128]{2,1,0:T(8,128)S(1)}, f32[72,384]{1,0:T(8,128)S(1)}) custom-call(s32[1,24]{1,0:T(1,128)} %bitcast.13, bf16[1088,128]{1,0:T(8,128)(2,1)S(1)} %bitcast.7), custom_call_target="tpu_custom_call" | custom-call | tf_op jit(solution)/shard_map/pallas_call | solution.py:197
  31.9 15.2 %all_to_all.21.in_ref = f32[16,16,128]{2,1,0:T(8,128)S(1)} all-to-all(f32[16,16,128]{2,1,0:T(8,128)S(1)} %get-tuple-element.6), channel_id=1, replica_groups=mesh['dp'=32,'mp'=16] {'mp'}, dimensions={0} | all-to-all | bytes 262144 | tf_op jit(solution)/shard_map/all_to_all | solution.py:212
  47.1 1.3 %shard_map.52 = (bf16[24,1024]{1,0:T(8,128)(2,1)}, bf16[1024,128]{1,0:T(8,128)(2,1)S(1)}) custom-call(f32[16,16,128]{2,1,0:T(8,128)S(1)} %all_to_all.21.in_ref, f32[72,384]{1,0:T(8,128)S(1)} %get-tuple-element.7.keep_ref), custom_call_target="tpu_custom_call" | custom-call | tf_op jit(solution)/shard_map/pallas_call | solution.py:197
  48.5 27.8 %all_to_all.22 = bf16[512,2,128]{2,1,0:T(2,128)(2,1)S(1)} all-to-all(bf16[512,2,128]{2,1,0:T(2,128)(2,1)S(1)} %bitcast.10), channel_id=1, replica_groups=mesh['dp'=32,'mp'=16] {'dp','mp'}, dimensions={0} | all-to-all | bytes 524288 | tf_op jit(solution)/shard_map/all_to_all | solution.py:212
  76.3 0.2 shard_map.53
  76.5 17.6 %all_to_all.23.in_ref = bf16[32,32,128]{2,1,0:T(8,128)(2,1)S(1)} all-to-all(bf16[32,32,128]{2,1,0:T(8,128)(2,1)S(1)} %shard_map.53), channel_id=1, replica_groups=mesh['dp'=32,'mp'=16] {'dp'}, dimensions={0} | all-to-all | bytes 524288 | tf_op jit(solution)/shard_map/all_to_all | solution.py:212
  94.1 1.0 %shard_map.54 = bf16[128,1024]{1,0:T(8,128)(2,1)} custom-call(bf16[32,32,128]{2,1,0:T(8,128)(2,1)S(1)} %all_to_all.23.in_ref), custom_call_target="tpu_custom_call" | custom-call | tf_op jit(solution)/shard_map/pallas_call | solution.py:197

commit v3 on v2

--- a/solution.py
+++ b/solution.py
@@ -24,6 +24,15 @@
 
 def iota(shape, dim):
     return lax.broadcasted_iota(i32, shape, dim)
+
+
+def rows_of(row, n):
+    one, zero = jnp.ones((), bf16), jnp.zeros((), bf16)
+    blocks = []
+    for at in range(0, n, 256):
+        number = iota((min(256, n - at), row.shape[1]), 0).astype(f32).astype(bf16)
+        blocks.append(jnp.where(number == (row - at).astype(bf16), one, zero))
+    return jnp.concatenate(blocks, axis=0)
 
 
 def hot(mask):
@@ -64,24 +73,25 @@
         ranks.append(jnp.sum(inside * (part[:, :width] + base), axis=0, keepdims=True))
         base = base + part[:, width:]
     rank = jnp.concatenate(ranks, axis=1).astype(i32)
-    r1 = rank & 3
-    r2 = rank >> 2
-    key = hot(iota((N_DP * 16, PTS), 0) == group * 16 + r2)
+    r1 = rank & 7
+    r2 = rank >> 3
+    key = rows_of((group * 8 + r2).astype(f32), N_DP * 8)
 
     line = iota((2 * N_DP, PTS), 0)
     digit = jnp.where((line & 1) == 0, local >> 3, local & 7).astype(f32)
     digit = jnp.where((line >> 1) == group, digit, 0.0).astype(bf16)
     turn = lax.axis_index("dp") * STRIDE
-    spot = (turn + (r1 >> 1) * 16 + r2 + 64 * (r1 & 1)) & 127
-    tags = dot_nt(digit, hot(iota((128, PTS), 0) == spot))
+    spot = (turn + (r1 >> 1) * 8 + r2 + 64 * (r1 & 1)) & 127
+    tags = dot_nt(digit, rows_of(spot.astype(f32), 128))
 
     fetch_points.wait()
     points = points_ref[...]
-    split = jnp.concatenate([points * hot(r1 == r) for r in range(4)], axis=0)
+    split = jnp.concatenate([points * hot(r1 == r) for r in range(8)], axis=0)
     moved = dot_nt(key, split)
     for d in range(N_DP):
-        rows_ref[STRIDE * d : STRIDE * d + 16, :] = moved[16 * d : 16 * d + 16, :128]
-        rows_ref[STRIDE * d + 16 : STRIDE * d + 32, :] = moved[16 * d : 16 * d + 16, 128:]
+        for h in range(4):
+            at = STRIDE * d + 8 * h
+            rows_ref[at : at + 8, :] = moved[8 * d : 8 * d + 8, 128 * h : 128 * (h + 1)]
         rows_ref[STRIDE * d + 32 : STRIDE * d + 34, :] = tags[2 * d : 2 * d + 2]
     out_ref[...] = rows_ref[...].astype(bf16)
 
@@ -106,8 +116,8 @@
             tile = jnp.where(source == iota((N_DP, 128), 0), tags, 0.0)
             tile = jnp.sum(tile, axis=0, keepdims=True)
             tiles.append(jnp.where((place - source * STRIDE)[:1] < 32, tile, -1.0))
-        label = jnp.concatenate(tiles, axis=1)[:, :total].astype(i32)
-        results.append(dot_nn(hot(iota((GROUP, total), 0) == label), data))
+        label = jnp.concatenate(tiles, axis=1)[:, :total]
+        results.append(dot_nn(rows_of(label, GROUP), data))
     left = iota((GROUP, 128), 1) < 64
     sums = jnp.where(left, results[0][:, :128], results[1][:, :128])
     sums = sums + pltpu.roll(sums, 64, 1)
@@ -157,7 +167,7 @@
     parent = jnp.concatenate(parent, axis=1).astype(i32)
     side = (parent >> 5) & 1
     device = (parent & 31) * N_MP + (parent >> 7)
-    key = hot(iota((2 * N_DP * N_MP, GROUP), 0) == device * 2 + ((parent >> 6) & 1))
+    key = rows_of((device * 2 + ((parent >> 6) & 1)).astype(f32), 2 * N_DP * N_MP)
 
     weighted = (keep_ref[0:64, :] * scale).astype(bf16).astype(f32) * keep_ref[64:65, :]
     both = jnp.concatenate(
@@ -165,7 +175,8 @@
     )
     high = both.astype(bf16)
     low = (both - high.astype(f32)).astype(bf16)
-    out_ref[...] = (dot_nt(key, high) + dot_nt(key, low)).astype(bf16)
+    total = dot_nt(key, jnp.concatenate([high, low], axis=0))
+    out_ref[...] = (total[:, :128] + total[:, 128:]).astype(bf16)
 
 
 def spread_kernel(in_ref, out_ref):
@@ -183,11 +194,12 @@
 
 
 def finish_kernel(in_ref, out_ref, rows_ref):
-    rows_ref[...] = in_ref[...].astype(f32).reshape(N_DP * 32, 128)
+    for i in range(N_DP):
+        rows_ref[33 * i : 33 * i + 32, :] = in_ref[i].astype(f32)
     for c in range(8):
         for q, r in enumerate((0, 2, 1, 3)):
             out_ref[32 * r : 32 * (r + 1), 128 * c : 128 * (c + 1)] = rows_ref[
-                pl.ds(4 * c + q, N_DP, stride=32), :
+                pl.ds(4 * c + q, N_DP, stride=33), :
             ].astype(bf16)
 
 
@@ -246,7 +258,7 @@
         finish_kernel,
         shape((K3_MP, D), bf16),
         exchange(parents, "dp"),
-        scratch=(pltpu.VMEM((N_DP * 32, 128), f32),),
+        scratch=(pltpu.VMEM((N_DP * 33, 128), f32),),
     )
     return (level2, level3)
 

time: 95.4 us -> 94.5 us (level)
  Pallas kernels: 6.43 us -> 5.46 us
    pallas_call x5, Pallas kernels: 6.43 us -> 5.46 us  [call(): pl.pallas_call(kernel, out_shape=out, in_specs=[pl.BlockSpec(memory_space...]
where the time goes in v3:
time: 94.5 us; the launch traced here: 94.2 us
  blocking collectives  88.1 us (93%)
  Pallas kernels  5.46 us (6%)
    all_to_all x4, blocking collectives, exchange(): return lax.all_to_all(x, axis, 0, 0, tiled=True)  88.1 us
    pallas_call x5, Pallas kernels, call(): pl.pallas_call(kernel, out_shape=out, in_specs=[pl.BlockSpec(memory_space...  5.46 us

profile of v3, /device:TPU:1, one launch (start us, length us, event | category | flops | bytes accessed | tf_op | source)
XLA Modules:
  0.0 94.2 jit_solution(3264670093921832449)
XLA Ops:
  0.6 2.3 %shard_map.50 = bf16[1088,128]{1,0:T(8,128)(2,1)S(1)} custom-call(s32[1,2048]{1,0:T(1,128)} %bitcast.12, bf16[64,2048]{1,0:T(8,128)(2,1)} %bitcast.11), custom_call_target="tpu_custom_call" | custom-call | tf_op jit(solution)/shard_map/pallas_call | solution.py:209
  2.9 27.4 %all_to_all.20 = bf16[32,17,2,128]{3,2,1,0:T(2,128)(2,1)S(1)} all-to-all(bf16[32,17,2,128]{3,2,1,0:T(2,128)(2,1)S(1)} %bitcast.8), channel_id=1, replica_groups=mesh['dp'=32,'mp'=16] {'dp'}, dimensions={0} | all-to-all | bytes 557056 | tf_op jit(solution)/shard_map/all_to_all | solution.py:224
  30.4 1.0 %shard_map.51 = (f32[16,16,128]{2,1,0:T(8,128)S(1)}, f32[72,384]{1,0:T(8,128)S(1)}) custom-call(s32[1,24]{1,0:T(1,128)} %bitcast.13, bf16[1088,128]{1,0:T(8,128)(2,1)S(1)} %bitcast.7), custom_call_target="tpu_custom_call" | custom-call | tf_op jit(solution)/shard_map/pallas_call | solution.py:209
  31.4 15.2 %all_to_all.21.in_ref = f32[16,16,128]{2,1,0:T(8,128)S(1)} all-to-all(f32[16,16,128]{2,1,0:T(8,128)S(1)} %get-tuple-element.6), channel_id=1, replica_groups=mesh['dp'=32,'mp'=16] {'mp'}, dimensions={0} | all-to-all | bytes 262144 | tf_op jit(solution)/shard_map/all_to_all | solution.py:224
  46.7 1.1 %shard_map.52 = (bf16[24,1024]{1,0:T(8,128)(2,1)}, bf16[1024,128]{1,0:T(8,128)(2,1)S(1)}) custom-call(f32[16,16,128]{2,1,0:T(8,128)S(1)} %all_to_all.21.in_ref, f32[72,384]{1,0:T(8,128)S(1)} %get-tuple-element.7.keep_ref), custom_call_target="tpu_custom_call" | custom-call | tf_op jit(solution)/shard_map/pallas_call | solution.py:209
  47.8 27.8 %all_to_all.22 = bf16[512,2,128]{2,1,0:T(2,128)(2,1)S(1)} all-to-all(bf16[512,2,128]{2,1,0:T(2,128)(2,1)S(1)} %bitcast.10), channel_id=1, replica_groups=mesh['dp'=32,'mp'=16] {'dp','mp'}, dimensions={0} | all-to-all | bytes 524288 | tf_op jit(solution)/shard_map/all_to_all | solution.py:224
  75.5 0.2 shard_map.53
  75.8 17.6 %all_to_all.23.in_ref = bf16[32,32,128]{2,1,0:T(8,128)(2,1)S(1)} all-to-all(bf16[32,32,128]{2,1,0:T(8,128)(2,1)S(1)} %shard_map.53), channel_id=1, replica_groups=mesh['dp'=32,'mp'=16] {'dp'}, dimensions={0} | all-to-all | bytes 524288 | tf_op jit(solution)/shard_map/all_to_all | solution.py:224
  93.4 0.8 shard_map.54

commit v4 on v3

v4 whole, which is shorter than its diff:
```python
import jax
import jax.numpy as jnp
from jax import lax
from jax.experimental import pallas as pl
from jax.experimental.pallas import tpu as pltpu
from jax.sharding import Mesh
from jax.sharding import PartitionSpec as P

N_DP = 32
N_MP = 16
PTS = 2048
FEAT = 64
ROWS = 24
GROUP = ROWS * N_MP
D = 1024
K3 = 2048
K3_MP = 128
EPS = 1e-06
STRIDE = 34

f32 = jnp.float32
bf16 = jnp.bfloat16
i32 = jnp.int32


def iota(shape, dim):
    return lax.broadcasted_iota(i32, shape, dim)


def rows_of(row, n):
    one, zero = jnp.ones((), bf16), jnp.zeros((), bf16)
    blocks = []
    for at in range(0, n, 256):
        number = iota((min(256, n - at), row.shape[1]), 0).astype(f32).astype(bf16)
        blocks.append(jnp.where(number == (row - at).astype(bf16), one, zero))
    return jnp.concatenate(blocks, axis=0)


def hot(mask):
    return jnp.where(mask, 1.0, 0.0).astype(bf16)


def dot_nt(a, b):
    return lax.dot_general(a, b, (((1,), (1,)), ((), ())), preferred_element_type=f32)


def dot_nn(a, b):
    return lax.dot_general(a, b, (((1,), (0,)), ((), ())), preferred_element_type=f32)


def sort_kernel(labels_hbm, points_hbm, out_ref, labels_ref, points_ref, rows_ref, sems):
    fetch_labels = pltpu.make_async_copy(labels_hbm, labels_ref, sems.at[0])
    fetch_points = pltpu.make_async_copy(points_hbm, points_ref, sems.at[1])
    fetch_labels.start()
    fetch_points.start()
    fetch_labels.wait()
    labels = labels_ref[...]
    group = ((labels >> 7) * 171) >> 9
    local = labels - group * GROUP
    member = jnp.where(iota((N_DP, PTS), 0) == group, 1.0, 0.0)
    member16 = member.astype(bf16)
    width = 256
    n_chunks = PTS // width
    stacked = jnp.concatenate(
        [member16[:, c * width : (c + 1) * width] for c in range(n_chunks)], axis=0
    )
    before = hot(iota((width, 2 * width), 0) < iota((width, 2 * width), 1))
    prefix = dot_nn(stacked, before)
    base = jnp.zeros((N_DP, width), f32)
    ranks = []
    for c in range(n_chunks):
        part = prefix[c * N_DP : (c + 1) * N_DP]
        inside = member[:, c * width : (c + 1) * width]
        ranks.append(jnp.sum(inside * (part[:, :width] + base), axis=0, keepdims=True))
        base = base + part[:, width:]
    rank = jnp.concatenate(ranks, axis=1).astype(i32)
    r1 = rank & 7
    r2 = rank >> 3
    key = rows_of((group * 8 + r2).astype(f32), N_DP * 8)

    line = iota((2 * N_DP, PTS), 0)
    digit = jnp.where((line & 1) == 0, local >> 3, local & 7).astype(f32)
    digit = jnp.where((line >> 2) == (group >> 1), digit, 0.0).astype(bf16)
    place = lax.axis_index("pair") * 2 + lax.axis_index("core")
    slot = (group & 1) * 4 + (r1 & 3)
    spot = (16 * (place + slot) + (r1 >> 2) * 8 + r2) & 127
    tags = dot_nt(digit, rows_of(spot.astype(f32), 128))

    fetch_points.wait()
    points = points_ref[...]
    masks = [hot(r1 == r) for r in range(8)]
    split = jnp.concatenate(
        [points[32 * half : 32 * half + 32] * masks[r] for half in range(2) for r in range(8)], axis=0
    )
    moved = dot_nt(key, split)
    for d in range(N_DP):
        pair, half = d >> 1, d & 1
        for own in range(2):
            for h in range(2):
                at = STRIDE * d + 16 * own + 8 * h
                line, lane = 8 * (2 * pair + own), 256 * half + 128 * h
                rows_ref[at : at + 8, :] = moved[line : line + 8, lane : lane + 128]
        rows_ref[STRIDE * d + 32 : STRIDE * d + 34, :] = tags[2 * d : 2 * d + 2]
    out_ref[...] = rows_ref[...].astype(bf16)


def sum_kernel(parent_hbm, in_ref, out_ref, keep_ref, parent_ref, rows_ref, sem):
    fetch = pltpu.make_async_copy(parent_hbm, parent_ref, sem)
    fetch.start()
    rows_ref[...] = in_ref[...].astype(f32)
    tags = 8.0 * rows_ref[pl.ds(32, N_DP, stride=STRIDE), :] + rows_ref[pl.ds(33, N_DP, stride=STRIDE), :]
    mine = iota((8, 128), 1) >> 4 == iota((8, 128), 0)
    quarter = iota((GROUP, 128), 1) >> 5
    half = N_DP * 16
    halves, squares = [], []
    for own in range(2):
        data = jnp.concatenate(
            [rows_ref[STRIDE * i + 16 * own : STRIDE * i + 16 * own + 16, :] for i in range(N_DP)], axis=0
        ).astype(bf16)
        data = jnp.concatenate([data, jnp.ones((half, 128), bf16)], axis=1)
        sums, counts = jnp.zeros((GROUP, 128), f32), jnp.zeros((GROUP, 128), f32)
        for s in range(4):
            slot = own * 4 + s
            turned = pltpu.roll(tags, 128 - 16 * slot, 1) if slot else tags
            label = jnp.concatenate(
                [
                    jnp.sum(jnp.where(mine, turned[8 * t : 8 * t + 8], 0.0), axis=0, keepdims=True)
                    for t in range(4)
                ],
                axis=1,
            )
            result = dot_nn(rows_of(label, GROUP), data)
            sums = jnp.where(quarter == s, result[:, :128], sums)
            counts = counts + result[:, 128:]
        sums = sums + pltpu.roll(sums, 64, 1)
        sums = sums + pltpu.roll(sums, 32, 1)
        turned = jnp.where(quarter == 0, sums, counts).T
        keep_ref[:, own * GROUP : (own + 1) * GROUP] = turned[:40]
        square = jnp.sum(turned[:32] * turned[:32], axis=0, keepdims=True)
        squares += [square[:, 128 * c : 128 * (c + 1)] for c in range(3)]
        sums = sums.reshape(N_MP, 3, 8, 128)
        band = iota((N_MP, 8, 128), 2) >> 5
        wide = jnp.where(band == 0, sums[:, 0], jnp.where(band == 1, sums[:, 1], sums[:, 2]))
        high = wide.astype(bf16)
        halves.append((high, (wide - high.astype(f32)).astype(bf16)))
    fetch.wait()
    parent = parent_ref[...]
    parent = jnp.concatenate([parent >> 3, parent & 7], axis=0).astype(f32)
    parent = jnp.concatenate([parent, jnp.zeros((2, 128 - ROWS), f32)], axis=1)
    tail = jnp.concatenate(squares + [parent], axis=0).astype(bf16)
    for own in range(2):
        block = slice(N_MP * own, N_MP * (own + 1))
        out_ref[block, 0:8, :] = halves[own][0]
        out_ref[block, 8:16, :] = halves[own][1]
    out_ref[:, 16:24, :] = jnp.broadcast_to(tail[None], (2 * N_MP, 8, 128))


def unit_kernel(in_ref, keep_ref, level2_ref, out_ref):
    band = iota((8, 128), 1) >> 5
    rows = ([], [], [])
    for c in range(N_MP // 2):
        parts = []
        for b in range(4):
            source = N_MP * (b & 1) + 2 * c + (b >> 1)
            parts.append(in_ref[source, 0:8, :].astype(f32) + in_ref[source, 8:16, :].astype(f32))
        for g in range(3):
            line = None
            for b in range(4):
                part = pltpu.roll(parts[b], (32 * (b - g)) % 128, 1) if b != g else parts[b]
                line = part if line is None else jnp.where(band == b, part, line)
            rows[g].append(line)
    lines = jnp.concatenate([jnp.concatenate(r, axis=1) for r in rows], axis=0)
    scale = lax.rsqrt(jnp.sum(lines * lines, axis=1, keepdims=True) * (1.0 / D) + EPS)
    level2_ref[...] = (lines * scale).astype(bf16)

    tails = in_ref[:, 16:24, :].astype(f32)
    squares = jnp.sum(tails, axis=0)
    squares = jnp.concatenate([squares[c : c + 1] for c in range(6)], axis=1)
    scale = lax.rsqrt(squares * (1.0 / D) + EPS)
    named = 8.0 * tails[:, 6:7] + tails[:, 7:8]
    named = jnp.concatenate(
        [pltpu.roll(named[n], (ROWS * n) % 128, 1) if n % N_MP else named[n] for n in range(2 * N_MP)], axis=0
    )
    parent = []
    for c in range(6):
        place = iota((2 * N_MP, 128), 1) + 128 * c
        mine = ((place >> 3) * 171) >> 9 == iota((2 * N_MP, 128), 0)
        parent.append(jnp.sum(jnp.where(mine, named, 0.0), axis=0, keepdims=True))
    parent = jnp.concatenate(parent, axis=1).astype(i32)
    device = ((parent >> 3) & 15) * N_MP + (parent >> 7)
    key = rows_of((device * 2 + (parent & 1)).astype(f32), N_DP * N_MP)

    weighted = (keep_ref[0:32, :] * scale).astype(bf16).astype(f32) * keep_ref[32:33, :]
    part = (parent >> 1) & 3
    both = jnp.concatenate([jnp.where(part == s, weighted, 0.0) for s in range(4)], axis=0)
    high = both.astype(bf16)
    low = (both - high.astype(f32)).astype(bf16)
    total = dot_nt(key, jnp.concatenate([high, low], axis=0))
    out_ref[...] = (total[:, :128] + total[:, 128:]).astype(bf16)


def spread_kernel(in_ref, out_ref):
    total = jnp.sum(in_ref[...].astype(f32).reshape(N_MP, 32, 128), axis=0).reshape(4, 8, 128)
    band, part = iota((4, 8, 128), 2) >> 5, iota((4, 8, 128), 1) >> 1
    turned = [total] + [pltpu.roll(total, 32 * d, 2) for d in range(1, 4)]
    out = jnp.zeros((4, 8, 128), f32)
    for b, j in enumerate((0, 2, 1, 3)):
        for s in range(4):
            piece = turned[(b - s) % 4]
            if s != j:
                piece = pltpu.roll(piece, (2 * (s - j)) % 8, 1)
            out = jnp.where((band == b) & (part == s), piece, out)
    out = jnp.where(lax.axis_index("core") == 1, pltpu.roll(out, 32, 2), out)
    out_ref[...] = jnp.broadcast_to(out.reshape(32, 128).astype(bf16)[None], (N_DP, 32, 128))


def finish_kernel(in_ref, out_ref):
    band = iota((N_MP, 8, 128), 2) >> 5
    tiles = []
    square = jnp.zeros((N_MP, 8, 128), f32)
    for t in range(4):
        block = pl.ds(8 * t, 8)
        first = jnp.concatenate([in_ref[2 * p : 2 * p + 1, block, :] for p in range(N_MP)], axis=0).astype(f32)
        second = jnp.concatenate([in_ref[2 * p + 1 : 2 * p + 2, block, :] for p in range(N_MP)], axis=0).astype(f32)
        even = (band & 1) == 0
        tiles.append(jnp.where(even, first, second))
        tiles.append(pltpu.roll(jnp.where(even, second, first), 96, 2))
        square = square + tiles[-1] * tiles[-1] + tiles[-2] * tiles[-2]
    scale = lax.rsqrt(jnp.sum(square, axis=2, keepdims=True) * (1.0 / D) + EPS)
    for c in range(8):
        out_ref[:, 128 * c : 128 * (c + 1)] = (tiles[c] * scale).reshape(K3_MP, 128).astype(bf16)


def call(kernel, out, *args, far=(), scratch=()):
    vmem = pl.BlockSpec(memory_space=pltpu.VMEM)
    many = isinstance(out, tuple)
    return pl.pallas_call(
        kernel,
        out_shape=out,
        in_specs=[pl.BlockSpec(memory_space=pltpu.HBM)] * len(far) + [vmem] * len(args),
        out_specs=(vmem,) * len(out) if many else vmem,
        scratch_shapes=scratch,
        compiler_params=pltpu.CompilerParams(vmem_limit_bytes=48 * 1024 * 1024),
    )(*(pltpu.with_memory_space_constraint(x, pltpu.HBM) for x in far), *args)


def shape(dims, dtype):
    return jax.ShapeDtypeStruct(dims, dtype)


def exchange(x, axis):
    return lax.all_to_all(x, axis, 0, 0, tiled=True)


def body(points, point_cluster, cluster_parent):
    rows = N_DP * STRIDE
    sent = call(
        sort_kernel,
        shape((rows, 128), bf16),
        far=(point_cluster.T, points.T),
        scratch=(
            pltpu.VMEM((1, PTS), i32),
            pltpu.VMEM((FEAT, PTS), bf16),
            pltpu.VMEM((rows, 128), f32),
            pltpu.SemaphoreType.DMA((2,)),
        ),
    )
    got = exchange(sent.reshape(N_DP, STRIDE // 2, 2, 128), ("pair", "core")).reshape(rows, 128)
    sums, keep = call(
        sum_kernel,
        (shape((2 * N_MP, 24, 128), bf16), shape((40, 2 * GROUP), f32)),
        got,
        far=(cluster_parent.T,),
        scratch=(
            pltpu.VMEM((1, ROWS), i32),
            pltpu.VMEM((rows, 128), f32),
            pltpu.SemaphoreType.DMA(()),
        ),
    )
    peers = N_DP // 2 * N_MP
    level2, partial = call(
        unit_kernel,
        (shape((ROWS, D), bf16), shape((2 * peers, 128), bf16)),
        exchange(sums, ("core", "mp")),
        keep,
    )
    parts = exchange(partial.reshape(peers, 2, 128), ("pair", "mp")).reshape(2 * peers, 128)
    parents = call(spread_kernel, shape((N_DP, 32, 128), bf16), parts)
    level3 = call(finish_kernel, shape((K3_MP, D), bf16), exchange(parents, ("pair", "core")))
    return (level2, level3)


def solution(mesh):
    pairs = Mesh(mesh.devices.reshape(N_DP // 2, 2, N_MP), ("pair", "core", "mp"))
    dp = ("pair", "core")
    placed = (P(dp, "mp"), P(dp, None), P((*dp, "mp"), None))
    return jax.shard_map(
        body,
        mesh=pairs,
        in_specs=placed,
        out_specs=(P((*dp, "mp"), None), P("mp", None)),
        check_vma=False,
    )
```

time: 94.5 us -> 93.1 us (0.985)
  blocking collectives: 88.1 us -> 85.7 us
  Pallas kernels: 5.46 us -> 6.42 us
    all_to_all x4, blocking collectives: 88.1 us -> 85.7 us  [exchange(): return lax.all_to_all(x, axis, 0, 0, tiled=True)]
    pallas_call x5, Pallas kernels: 5.46 us -> 6.42 us  [call(): pl.pallas_call(kernel, out_shape=out, in_specs=[pl.BlockSpec(memory_space...]
where the time goes in v4:
time: 93.1 us; the launch traced here: 92.8 us
  blocking collectives  85.7 us (92%)
  Pallas kernels  6.42 us (7%)
    all_to_all x4, blocking collectives, exchange(): return lax.all_to_all(x, axis, 0, 0, tiled=True)  85.7 us
    pallas_call x5, Pallas kernels, call(): pl.pallas_call(kernel, out_shape=out, in_specs=[pl.BlockSpec(memory_space...  6.42 us

profile of v4, /device:TPU:1, one launch (start us, length us, event | category | flops | bytes accessed | tf_op | source)
XLA Modules:
  0.0 92.8 jit_solution(10749733421792220679)
XLA Ops:
  0.6 2.4 %shard_map.50 = bf16[1088,128]{1,0:T(8,128)(2,1)S(1)} custom-call(s32[1,2048]{1,0:T(1,128)} %bitcast.12, bf16[64,2048]{1,0:T(8,128)(2,1)} %bitcast.11), custom_call_target="tpu_custom_call" | custom-call | tf_op jit(solution)/shard_map/pallas_call | solution.py:237
  3.0 27.4 %all_to_all.20 = bf16[32,17,2,128]{3,2,1,0:T(2,128)(2,1)S(1)} all-to-all(bf16[32,17,2,128]{3,2,1,0:T(2,128)(2,1)S(1)} %bitcast.8), channel_id=1, replica_groups=mesh['pair'=16,'core'=2,'mp'=16] {'pair','core'}, dimensions={0} | all-to-all | bytes 557056 | tf_op jit(solution)/shard_map/all_to_all | solution.py:252
  30.5 1.8 %shard_map.51 = (bf16[32,24,128]{2,1,0:T(8,128)(2,1)S(1)}, f32[40,768]{1,0:T(8,128)S(1)}) custom-call(s32[1,24]{1,0:T(1,128)} %bitcast.13, bf16[1088,128]{1,0:T(8,128)(2,1)S(1)} %bitcast.7), custom_call_target="tpu_custom_call" | custom-call | tf_op jit(solution)/shard_map/pallas_call | solution.py:237
  32.3 18.2 %all_to_all.21.in_ref = bf16[32,24,128]{2,1,0:T(8,128)(2,1)S(1)} all-to-all(bf16[32,24,128]{2,1,0:T(8,128)(2,1)S(1)} %get-tuple-element.6), channel_id=1, replica_groups=mesh['pair'=16,'core'=2,'mp'=16] {'core','mp'}, dimensions={0} | all-to-all | bytes 393216 | tf_op jit(solution)/shard_map/all_to_all | solution.py:252
  50.5 1.1 %shard_map.52 = (bf16[24,1024]{1,0:T(8,128)(2,1)}, bf16[512,128]{1,0:T(8,128)(2,1)S(1)}) custom-call(bf16[32,24,128]{2,1,0:T(8,128)(2,1)S(1)} %all_to_all.21.in_ref, f32[40,768]{1,0:T(8,128)S(1)} %get-tuple-element.7.keep_ref), custom_call_target="tpu_custom_call" | custom-call | tf_op jit(solution)/shard_map/pallas_call | solution.py:237
  51.6 21.3 %all_to_all.22 = bf16[256,2,128]{2,1,0:T(2,128)(2,1)S(1)} all-to-all(bf16[256,2,128]{2,1,0:T(2,128)(2,1)S(1)} %bitcast.10), channel_id=1, replica_groups=mesh['pair'=16,'core'=2,'mp'=16] {'pair','mp'}, dimensions={0} | all-to-all | bytes 262144 | tf_op jit(solution)/shard_map/all_to_all | solution.py:252
  72.9 0.2 shard_map.53
  73.1 18.7 %all_to_all.23.in_ref = bf16[32,32,128]{2,1,0:T(8,128)(2,1)S(1)} all-to-all(bf16[32,32,128]{2,1,0:T(8,128)(2,1)S(1)} %shard_map.53), channel_id=1, replica_groups=mesh['pair'=16,'core'=2,'mp'=16] {'pair','core'}, dimensions={0} | all-to-all | bytes 524288 | tf_op jit(solution)/shard_map/all_to_all | solution.py:252
  91.8 0.9 %shard_map.54 = bf16[128,1024]{1,0:T(8,128)(2,1)} custom-call(bf16[32,32,128]{2,1,0:T(8,128)(2,1)S(1)} %all_to_all.23.in_ref), custom_call_target="tpu_custom_call" | custom-call | tf_op jit(solution)/shard_map/pallas_call | solution.py:237

commit v5 on v4

--- a/solution.py
+++ b/solution.py
@@ -112,26 +112,24 @@
     mine = iota((8, 128), 1) >> 4 == iota((8, 128), 0)
     quarter = iota((GROUP, 128), 1) >> 5
     half = N_DP * 16
-    halves, squares = [], []
+    sides = [hot(iota((1, 128), 1) >> 5 == s) for s in range(4)]
+    wides, squares = [], []
     for own in range(2):
         data = jnp.concatenate(
             [rows_ref[STRIDE * i + 16 * own : STRIDE * i + 16 * own + 16, :] for i in range(N_DP)], axis=0
         ).astype(bf16)
-        data = jnp.concatenate([data, jnp.ones((half, 128), bf16)], axis=1)
-        sums, counts = jnp.zeros((GROUP, 128), f32), jnp.zeros((GROUP, 128), f32)
+        labels = []
         for s in range(4):
             slot = own * 4 + s
             turned = pltpu.roll(tags, 128 - 16 * slot, 1) if slot else tags
-            label = jnp.concatenate(
-                [
-                    jnp.sum(jnp.where(mine, turned[8 * t : 8 * t + 8], 0.0), axis=0, keepdims=True)
-                    for t in range(4)
-                ],
-                axis=1,
-            )
-            result = dot_nn(rows_of(label, GROUP), data)
-            sums = jnp.where(quarter == s, result[:, :128], sums)
-            counts = counts + result[:, 128:]
+            labels += [
+                jnp.sum(jnp.where(mine, turned[8 * t : 8 * t + 8], 0.0), axis=0, keepdims=True)
+                for t in range(4)
+            ]
+        split = jnp.concatenate([data * side for side in sides], axis=0)
+        split = jnp.concatenate([split, jnp.ones((4 * half, 128), bf16)], axis=1)
+        result = dot_nn(rows_of(jnp.concatenate(labels, axis=1), GROUP), split)
+        sums, counts = result[:, :128], result[:, 128:]
         sums = sums + pltpu.roll(sums, 64, 1)
         sums = sums + pltpu.roll(sums, 32, 1)
         turned = jnp.where(quarter == 0, sums, counts).T
@@ -141,8 +139,7 @@
         sums = sums.reshape(N_MP, 3, 8, 128)
         band = iota((N_MP, 8, 128), 2) >> 5
         wide = jnp.where(band == 0, sums[:, 0], jnp.where(band == 1, sums[:, 1], sums[:, 2]))
-        high = wide.astype(bf16)
-        halves.append((high, (wide - high.astype(f32)).astype(bf16)))
+        wides.append(wide.astype(bf16))
     fetch.wait()
     parent = parent_ref[...]
     parent = jnp.concatenate([parent >> 3, parent & 7], axis=0).astype(f32)
@@ -150,9 +147,8 @@
     tail = jnp.concatenate(squares + [parent], axis=0).astype(bf16)
     for own in range(2):
         block = slice(N_MP * own, N_MP * (own + 1))
-        out_ref[block, 0:8, :] = halves[own][0]
-        out_ref[block, 8:16, :] = halves[own][1]
-    out_ref[:, 16:24, :] = jnp.broadcast_to(tail[None], (2 * N_MP, 8, 128))
+        out_ref[block, 0:8, :] = wides[own]
+    out_ref[:, 8:16, :] = jnp.broadcast_to(tail[None], (2 * N_MP, 8, 128))
 
 
 def unit_kernel(in_ref, keep_ref, level2_ref, out_ref):
@@ -162,7 +158,7 @@
         parts = []
         for b in range(4):
             source = N_MP * (b & 1) + 2 * c + (b >> 1)
-            parts.append(in_ref[source, 0:8, :].astype(f32) + in_ref[source, 8:16, :].astype(f32))
+            parts.append(in_ref[source, 0:8, :].astype(f32))
         for g in range(3):
             line = None
             for b in range(4):
@@ -173,7 +169,7 @@
     scale = lax.rsqrt(jnp.sum(lines * lines, axis=1, keepdims=True) * (1.0 / D) + EPS)
     level2_ref[...] = (lines * scale).astype(bf16)
 
-    tails = in_ref[:, 16:24, :].astype(f32)
+    tails = in_ref[:, 8:16, :].astype(f32)
     squares = jnp.sum(tails, axis=0)
     squares = jnp.concatenate([squares[c : c + 1] for c in range(6)], axis=1)
     scale = lax.rsqrt(squares * (1.0 / D) + EPS)
@@ -268,7 +264,7 @@
     got = exchange(sent.reshape(N_DP, STRIDE // 2, 2, 128), ("pair", "core")).reshape(rows, 128)
     sums, keep = call(
         sum_kernel,
-        (shape((2 * N_MP, 24, 128), bf16), shape((40, 2 * GROUP), f32)),
+        (shape((2 * N_MP, 16, 128), bf16), shape((40, 2 * GROUP), f32)),
         got,
         far=(cluster_parent.T,),
         scratch=(

time: 93.1 us -> 91.2 us (0.980)
  blocking collectives: 85.7 us -> 84.3 us
    all_to_all x4, blocking collectives: 85.7 us -> 84.3 us  [exchange(): return lax.all_to_all(x, axis, 0, 0, tiled=True)]
where the time goes in v5:
time: 91.2 us; the launch traced here: 90.9 us
  blocking collectives  84.3 us (92%)
  Pallas kernels  5.97 us (7%)
    all_to_all x4, blocking collectives, exchange(): return lax.all_to_all(x, axis, 0, 0, tiled=True)  84.3 us
    pallas_call x5, Pallas kernels, call(): pl.pallas_call(kernel, out_shape=out, in_specs=[pl.BlockSpec(memory_space...  5.97 us

profile of v5, /device:TPU:1, one launch (start us, length us, event | category | flops | bytes accessed | tf_op | source)
XLA Modules:
  0.0 90.9 jit_solution(17073030733551240840)
XLA Ops:
  0.6 2.4 %shard_map.50 = bf16[1088,128]{1,0:T(8,128)(2,1)S(1)} custom-call(s32[1,2048]{1,0:T(1,128)} %bitcast.12, bf16[64,2048]{1,0:T(8,128)(2,1)} %bitcast.11), custom_call_target="tpu_custom_call" | custom-call | tf_op jit(solution)/shard_map/pallas_call | solution.py:233
  3.0 27.4 %all_to_all.20 = bf16[32,17,2,128]{3,2,1,0:T(2,128)(2,1)S(1)} all-to-all(bf16[32,17,2,128]{3,2,1,0:T(2,128)(2,1)S(1)} %bitcast.8), channel_id=1, replica_groups=mesh['pair'=16,'core'=2,'mp'=16] {'pair','core'}, dimensions={0} | all-to-all | bytes 557056 | tf_op jit(solution)/shard_map/all_to_all | solution.py:248
  30.5 1.4 %shard_map.51 = (bf16[32,16,128]{2,1,0:T(8,128)(2,1)S(1)}, f32[40,768]{1,0:T(8,128)S(1)}) custom-call(s32[1,24]{1,0:T(1,128)} %bitcast.13, bf16[1088,128]{1,0:T(8,128)(2,1)S(1)} %bitcast.7), custom_call_target="tpu_custom_call" | custom-call | tf_op jit(solution)/shard_map/pallas_call | solution.py:233
  31.8 16.9 %all_to_all.21.in_ref = bf16[32,16,128]{2,1,0:T(8,128)(2,1)S(1)} all-to-all(bf16[32,16,128]{2,1,0:T(8,128)(2,1)S(1)} %get-tuple-element.6), channel_id=1, replica_groups=mesh['pair'=16,'core'=2,'mp'=16] {'core','mp'}, dimensions={0} | all-to-all | bytes 262144 | tf_op jit(solution)/shard_map/all_to_all | solution.py:248
  48.7 1.1 %shard_map.52 = (bf16[24,1024]{1,0:T(8,128)(2,1)}, bf16[512,128]{1,0:T(8,128)(2,1)S(1)}) custom-call(bf16[32,16,128]{2,1,0:T(8,128)(2,1)S(1)} %all_to_all.21.in_ref, f32[40,768]{1,0:T(8,128)S(1)} %get-tuple-element.7.keep_ref), custom_call_target="tpu_custom_call" | custom-call | tf_op jit(solution)/shard_map/pallas_call | solution.py:233
  49.8 21.2 %all_to_all.22 = bf16[256,2,128]{2,1,0:T(2,128)(2,1)S(1)} all-to-all(bf16[256,2,128]{2,1,0:T(2,128)(2,1)S(1)} %bitcast.10), channel_id=1, replica_groups=mesh['pair'=16,'core'=2,'mp'=16] {'pair','mp'}, dimensions={0} | all-to-all | bytes 262144 | tf_op jit(solution)/shard_map/all_to_all | solution.py:248
  71.1 0.2 shard_map.53
  71.3 18.7 %all_to_all.23.in_ref = bf16[32,32,128]{2,1,0:T(8,128)(2,1)S(1)} all-to-all(bf16[32,32,128]{2,1,0:T(8,128)(2,1)S(1)} %shard_map.53), channel_id=1, replica_groups=mesh['pair'=16,'core'=2,'mp'=16] {'pair','core'}, dimensions={0} | all-to-all | bytes 524288 | tf_op jit(solution)/shard_map/all_to_all | solution.py:248
  90.0 0.9 %shard_map.54 = bf16[128,1024]{1,0:T(8,128)(2,1)} custom-call(bf16[32,32,128]{2,1,0:T(8,128)(2,1)S(1)} %all_to_all.23.in_ref), custom_call_target="tpu_custom_call" | custom-call | tf_op jit(solution)/shard_map/pallas_call | solution.py:233

commit v6 on v5

--- a/solution.py
+++ b/solution.py
@@ -78,13 +78,12 @@
     r2 = rank >> 3
     key = rows_of((group * 8 + r2).astype(f32), N_DP * 8)
 
-    line = iota((2 * N_DP, PTS), 0)
+    line = iota((N_DP, PTS), 0)
     digit = jnp.where((line & 1) == 0, local >> 3, local & 7).astype(f32)
-    digit = jnp.where((line >> 2) == (group >> 1), digit, 0.0).astype(bf16)
+    digit = jnp.where((line >> 1) == (group >> 1), digit, 0.0).astype(bf16)
     place = lax.axis_index("pair") * 2 + lax.axis_index("core")
     slot = (group & 1) * 4 + (r1 & 3)
     spot = (16 * (place + slot) + (r1 >> 2) * 8 + r2) & 127
-    tags = dot_nt(digit, rows_of(spot.astype(f32), 128))
 
     fetch_points.wait()
     points = points_ref[...]
@@ -93,6 +92,7 @@
         [points[32 * half : 32 * half + 32] * masks[r] for half in range(2) for r in range(8)], axis=0
     )
     moved = dot_nt(key, split)
+    tags = dot_nt(digit, rows_of(spot.astype(f32), 128))
     for d in range(N_DP):
         pair, half = d >> 1, d & 1
         for own in range(2):
@@ -100,7 +100,7 @@
                 at = STRIDE * d + 16 * own + 8 * h
                 line, lane = 8 * (2 * pair + own), 256 * half + 128 * h
                 rows_ref[at : at + 8, :] = moved[line : line + 8, lane : lane + 128]
-        rows_ref[STRIDE * d + 32 : STRIDE * d + 34, :] = tags[2 * d : 2 * d + 2]
+        rows_ref[STRIDE * d + 32 : STRIDE * d + 34, :] = tags[2 * pair : 2 * pair + 2]
     out_ref[...] = rows_ref[...].astype(bf16)
 
 
@@ -210,7 +210,9 @@
     out_ref[...] = jnp.broadcast_to(out.reshape(32, 128).astype(bf16)[None], (N_DP, 32, 128))
 
 
-def finish_kernel(in_ref, out_ref):
+def finish_kernel(in_ref, level2_ref, out_hbm, level2_hbm, out_ref, sems):
+    stores = [pltpu.make_async_copy(level2_ref, level2_hbm, sems.at[2])]
+    stores[0].start()
     band = iota((N_MP, 8, 128), 2) >> 5
     tiles = []
     square = jnp.zeros((N_MP, 8, 128), f32)
@@ -223,18 +225,26 @@
         tiles.append(pltpu.roll(jnp.where(even, second, first), 96, 2))
         square = square + tiles[-1] * tiles[-1] + tiles[-2] * tiles[-2]
     scale = lax.rsqrt(jnp.sum(square, axis=2, keepdims=True) * (1.0 / D) + EPS)
-    for c in range(8):
-        out_ref[:, 128 * c : 128 * (c + 1)] = (tiles[c] * scale).reshape(K3_MP, 128).astype(bf16)
-
-
-def call(kernel, out, *args, far=(), scratch=()):
-    vmem = pl.BlockSpec(memory_space=pltpu.VMEM)
+    for n in range(2):
+        block = pl.ds(64 * n, 64)
+        for c in range(8):
+            part = tiles[c][8 * n : 8 * n + 8] * scale[8 * n : 8 * n + 8]
+            out_ref[block, 128 * c : 128 * (c + 1)] = part.reshape(64, 128).astype(bf16)
+        stores.append(pltpu.make_async_copy(out_ref.at[block], out_hbm.at[block], sems.at[n]))
+        stores[-1].start()
+    for store in stores:
+        store.wait()
+
+
+def call(kernel, out, *args, far=(), scratch=(), spaces=(pltpu.VMEM,)):
     many = isinstance(out, tuple)
+    results = tuple(pl.BlockSpec(memory_space=space) for space in spaces)
     return pl.pallas_call(
         kernel,
         out_shape=out,
-        in_specs=[pl.BlockSpec(memory_space=pltpu.HBM)] * len(far) + [vmem] * len(args),
-        out_specs=(vmem,) * len(out) if many else vmem,
+        in_specs=[pl.BlockSpec(memory_space=pltpu.HBM)] * len(far)
+        + [pl.BlockSpec(memory_space=pltpu.VMEM)] * len(args),
+        out_specs=results if many else results[0],
         scratch_shapes=scratch,
         compiler_params=pltpu.CompilerParams(vmem_limit_bytes=48 * 1024 * 1024),
     )(*(pltpu.with_memory_space_constraint(x, pltpu.HBM) for x in far), *args)
@@ -272,6 +282,7 @@
             pltpu.VMEM((rows, 128), f32),
             pltpu.SemaphoreType.DMA(()),
         ),
+        spaces=(pltpu.VMEM, pltpu.VMEM),
     )
     peers = N_DP // 2 * N_MP
     level2, partial = call(
@@ -279,10 +290,18 @@
         (shape((ROWS, D), bf16), shape((2 * peers, 128), bf16)),
         exchange(sums, ("core", "mp")),
         keep,
+        spaces=(pltpu.VMEM, pltpu.VMEM),
     )
     parts = exchange(partial.reshape(peers, 2, 128), ("pair", "mp")).reshape(2 * peers, 128)
     parents = call(spread_kernel, shape((N_DP, 32, 128), bf16), parts)
-    level3 = call(finish_kernel, shape((K3_MP, D), bf16), exchange(parents, ("pair", "core")))
+    level3, level2 = call(
+        finish_kernel,
+        (shape((K3_MP, D), bf16), shape((ROWS, D), bf16)),
+        exchange(parents, ("pair", "core")),
+        level2,
+        scratch=(pltpu.VMEM((K3_MP, D), bf16), pltpu.SemaphoreType.DMA((3,))),
+        spaces=(pltpu.HBM, pltpu.HBM),
+    )
     return (level2, level3)
 
 

time: 91.2 us -> 90.4 us (level)
  no operation moved by 1% of the time
where the time goes in v6:
time: 90.4 us; the launch traced here: 90.1 us
  blocking collectives  84.3 us (93%)
  Pallas kernels  5.13 us (6%)
    all_to_all x4, blocking collectives, exchange(): return lax.all_to_all(x, axis, 0, 0, tiled=True)  84.3 us
    pallas_call x5, Pallas kernels, call(): pl.pallas_call(kernel, out_shape=out, in_specs=[pl.BlockSpec(memory_space...  5.13 us

profile of v6, /device:TPU:1, one launch (start us, length us, event | category | flops | bytes accessed | tf_op | source)
XLA Modules:
  0.0 90.1 jit_solution(5154062837056247077)
XLA Ops:
  0.6 2.1 %shard_map.50 = bf16[1088,128]{1,0:T(8,128)(2,1)S(1)} custom-call(s32[1,2048]{1,0:T(1,128)} %bitcast.12, bf16[64,2048]{1,0:T(8,128)(2,1)} %bitcast.11), custom_call_target="tpu_custom_call" | custom-call | tf_op jit(solution)/shard_map/pallas_call | solution.py:242
  2.7 27.4 %all_to_all.20 = bf16[32,17,2,128]{3,2,1,0:T(2,128)(2,1)S(1)} all-to-all(bf16[32,17,2,128]{3,2,1,0:T(2,128)(2,1)S(1)} %bitcast.8), channel_id=1, replica_groups=mesh['pair'=16,'core'=2,'mp'=16] {'pair','core'}, dimensions={0} | all-to-all | bytes 557056 | tf_op jit(solution)/shard_map/all_to_all | solution.py:258
  30.2 1.4 %shard_map.51 = (bf16[32,16,128]{2,1,0:T(8,128)(2,1)S(1)}, f32[40,768]{1,0:T(8,128)S(1)}) custom-call(s32[1,24]{1,0:T(1,128)} %bitcast.13, bf16[1088,128]{1,0:T(8,128)(2,1)S(1)} %bitcast.7), custom_call_target="tpu_custom_call" | custom-call | tf_op jit(solution)/shard_map/pallas_call | solution.py:242
  31.6 16.9 %all_to_all.21.in_ref = bf16[32,16,128]{2,1,0:T(8,128)(2,1)S(1)} all-to-all(bf16[32,16,128]{2,1,0:T(8,128)(2,1)S(1)} %get-tuple-element.8), channel_id=1, replica_groups=mesh['pair'=16,'core'=2,'mp'=16] {'core','mp'}, dimensions={0} | all-to-all | bytes 262144 | tf_op jit(solution)/shard_map/all_to_all | solution.py:258
  48.5 0.5 shard_map.52
  49.0 21.3 %all_to_all.22 = bf16[256,2,128]{2,1,0:T(2,128)(2,1)S(1)} all-to-all(bf16[256,2,128]{2,1,0:T(2,128)(2,1)S(1)} %bitcast.10), channel_id=1, replica_groups=mesh['pair'=16,'core'=2,'mp'=16] {'pair','mp'}, dimensions={0} | all-to-all | bytes 262144 | tf_op jit(solution)/shard_map/all_to_all | solution.py:258
  70.3 0.2 shard_map.53
  70.5 18.7 %all_to_all.23.in_ref = bf16[32,32,128]{2,1,0:T(8,128)(2,1)S(1)} all-to-all(bf16[32,32,128]{2,1,0:T(8,128)(2,1)S(1)} %shard_map.53), channel_id=1, replica_groups=mesh['pair'=16,'core'=2,'mp'=16] {'pair','core'}, dimensions={0} | all-to-all | bytes 524288 | tf_op jit(solution)/shard_map/all_to_all | solution.py:258
  89.1 0.9 %shard_map.54 = (bf16[128,1024]{1,0:T(8,128)(2,1)}, bf16[24,1024]{1,0:T(8,128)(2,1)}) custom-call(bf16[32,32,128]{2,1,0:T(8,128)(2,1)S(1)} %all_to_all.23.in_ref, bf16[24,1024]{1,0:T(8,128)(2,1)S(1)} %get-tuple-element.11.level2_ref), custom_call_target="tpu_custom_call" | custom-call | tf_op jit(solution)/shard_map/pallas_call | solution.py:242

commit v7 on v6

--- a/solution.py
+++ b/solution.py
@@ -104,7 +104,7 @@
     out_ref[...] = rows_ref[...].astype(bf16)
 
 
-def sum_kernel(parent_hbm, in_ref, out_ref, keep_ref, parent_ref, rows_ref, sem):
+def sum_kernel(parent_hbm, in_ref, out_ref, keep_ref, count_ref, parent_ref, rows_ref, sem):
     fetch = pltpu.make_async_copy(parent_hbm, parent_ref, sem)
     fetch.start()
     rows_ref[...] = in_ref[...].astype(f32)
@@ -133,7 +133,8 @@
         sums = sums + pltpu.roll(sums, 64, 1)
         sums = sums + pltpu.roll(sums, 32, 1)
         turned = jnp.where(quarter == 0, sums, counts).T
-        keep_ref[:, own * GROUP : (own + 1) * GROUP] = turned[:40]
+        keep_ref[:, own * GROUP : (own + 1) * GROUP] = turned[:32]
+        count_ref[:, own * GROUP : (own + 1) * GROUP] = turned[32:40]
         square = jnp.sum(turned[:32] * turned[:32], axis=0, keepdims=True)
         squares += [square[:, 128 * c : 128 * (c + 1)] for c in range(3)]
         sums = sums.reshape(N_MP, 3, 8, 128)
@@ -151,7 +152,7 @@
     out_ref[:, 8:16, :] = jnp.broadcast_to(tail[None], (2 * N_MP, 8, 128))
 
 
-def unit_kernel(in_ref, keep_ref, level2_ref, out_ref):
+def unit_kernel(in_ref, keep_ref, other_ref, count_ref, level2_ref, out_ref):
     band = iota((8, 128), 1) >> 5
     rows = ([], [], [])
     for c in range(N_MP // 2):
@@ -183,12 +184,23 @@
         mine = ((place >> 3) * 171) >> 9 == iota((2 * N_MP, 128), 0)
         parent.append(jnp.sum(jnp.where(mine, named, 0.0), axis=0, keepdims=True))
     parent = jnp.concatenate(parent, axis=1).astype(i32)
-    device = ((parent >> 3) & 15) * N_MP + (parent >> 7)
-    key = rows_of((device * 2 + (parent & 1)).astype(f32), N_DP * N_MP)
-
-    weighted = (keep_ref[0:32, :] * scale).astype(bf16).astype(f32) * keep_ref[32:33, :]
-    part = (parent >> 1) & 3
-    both = jnp.concatenate([jnp.where(part == s, weighted, 0.0) for s in range(4)], axis=0)
+    side = lax.axis_index("xl")
+    line = (((parent >> 3) & 15) * 8 + (parent >> 8)) * 4 + (parent & 3)
+    line = jnp.where(((parent >> 7) & 1) == side, line, -1)
+    key = rows_of(line.astype(f32), N_DP * N_MP)
+
+    factor = count_ref[0:1, :]
+    own = (keep_ref[...] * scale).astype(bf16).astype(f32) * factor
+    other = (other_ref[...] * scale).astype(bf16).astype(f32) * factor
+    part = (parent >> 2) & 1
+    both = jnp.concatenate(
+        [
+            jnp.where(part == s, block, 0.0)
+            for block in (jnp.where(side == 0, own, other), jnp.where(side == 0, other, own))
+            for s in range(2)
+        ],
+        axis=0,
+    )
     high = both.astype(bf16)
     low = (both - high.astype(f32)).astype(bf16)
     total = dot_nt(key, jnp.concatenate([high, low], axis=0))
@@ -196,16 +208,11 @@
 
 
 def spread_kernel(in_ref, out_ref):
-    total = jnp.sum(in_ref[...].astype(f32).reshape(N_MP, 32, 128), axis=0).reshape(4, 8, 128)
-    band, part = iota((4, 8, 128), 2) >> 5, iota((4, 8, 128), 1) >> 1
-    turned = [total] + [pltpu.roll(total, 32 * d, 2) for d in range(1, 4)]
-    out = jnp.zeros((4, 8, 128), f32)
-    for b, j in enumerate((0, 2, 1, 3)):
-        for s in range(4):
-            piece = turned[(b - s) % 4]
-            if s != j:
-                piece = pltpu.roll(piece, (2 * (s - j)) % 8, 1)
-            out = jnp.where((band == b) & (part == s), piece, out)
+    total = jnp.sum(in_ref[...].astype(f32).reshape(N_DP // 2, 32, 128), axis=0).reshape(4, 8, 128)
+    odd, lower = (iota((4, 8, 128), 2) >> 5) & 1, iota((4, 8, 128), 1) >> 2
+    swapped = pltpu.roll(total, 4, 1)
+    swapped = jnp.where(lower == 0, pltpu.roll(swapped, 32, 2), pltpu.roll(swapped, 96, 2))
+    out = jnp.where(odd == lower, total, swapped)
     out = jnp.where(lax.axis_index("core") == 1, pltpu.roll(out, 32, 2), out)
     out_ref[...] = jnp.broadcast_to(out.reshape(32, 128).astype(bf16)[None], (N_DP, 32, 128))
 
@@ -272,9 +279,9 @@
         ),
     )
     got = exchange(sent.reshape(N_DP, STRIDE // 2, 2, 128), ("pair", "core")).reshape(rows, 128)
-    sums, keep = call(
+    sums, keep, counts = call(
         sum_kernel,
-        (shape((2 * N_MP, 16, 128), bf16), shape((40, 2 * GROUP), f32)),
+        (shape((2 * N_MP, 16, 128), bf16), shape((32, 2 * GROUP), f32), shape((8, 2 * GROUP), f32)),
         got,
         far=(cluster_parent.T,),
         scratch=(
@@ -282,17 +289,20 @@
             pltpu.VMEM((rows, 128), f32),
             pltpu.SemaphoreType.DMA(()),
         ),
-        spaces=(pltpu.VMEM, pltpu.VMEM),
-    )
-    peers = N_DP // 2 * N_MP
+        spaces=(pltpu.VMEM,) * 3,
+    )
+    other = lax.ppermute(keep, "xl", [(0, 1), (1, 0)])
+    peers = N_DP // 2 * N_MP // 2
     level2, partial = call(
         unit_kernel,
-        (shape((ROWS, D), bf16), shape((2 * peers, 128), bf16)),
-        exchange(sums, ("core", "mp")),
+        (shape((ROWS, D), bf16), shape((4 * peers, 128), bf16)),
+        exchange(sums, ("core", "y", "xl")),
         keep,
+        other,
+        counts,
         spaces=(pltpu.VMEM, pltpu.VMEM),
     )
-    parts = exchange(partial.reshape(peers, 2, 128), ("pair", "mp")).reshape(2 * peers, 128)
+    parts = exchange(partial.reshape(peers, 4, 128), ("pair", "y")).reshape(4 * peers, 128)
     parents = call(spread_kernel, shape((N_DP, 32, 128), bf16), parts)
     level3, level2 = call(
         finish_kernel,
@@ -306,13 +316,13 @@
 
 
 def solution(mesh):
-    pairs = Mesh(mesh.devices.reshape(N_DP // 2, 2, N_MP), ("pair", "core", "mp"))
-    dp = ("pair", "core")
-    placed = (P(dp, "mp"), P(dp, None), P((*dp, "mp"), None))
+    split = Mesh(mesh.devices.reshape(N_DP // 2, 2, N_MP // 2, 2), ("pair", "core", "y", "xl"))
+    dp, mp = ("pair", "core"), ("y", "xl")
+    placed = (P(dp, mp), P(dp, None), P((*dp, *mp), None))
     return jax.shard_map(
         body,
-        mesh=pairs,
+        mesh=split,
         in_specs=placed,
-        out_specs=(P((*dp, "mp"), None), P("mp", None)),
+        out_specs=(P((*dp, *mp), None), P(mp, None)),
         check_vma=False,
     )

time: 90.4 us -> 90.7 us (level)
  blocking collectives: 84.3 us -> 66.8 us
  starting transfers between devices: 0 us -> 11 us
  waiting for transfers between devices: 0 us -> 6.06 us
    all_to_all x4 -> x3, blocking collectives: 84.3 us -> 66.8 us  [exchange(): return lax.all_to_all(x, axis, 0, 0, tiled=True)]
    all_to_all x0 -> x1, starting transfers between devices: none -> 7.76 us  [exchange(): return lax.all_to_all(x, axis, 0, 0, tiled=True)]
    ppermute x0 -> x1, waiting for transfers between devices: none -> 3.71 us  [body(): other = lax.ppermute(keep, 'xl', [(0, 1), (1, 0)])]
    ppermute x0 -> x1, starting transfers between devices: none -> 3.29 us  [body(): other = lax.ppermute(keep, 'xl', [(0, 1), (1, 0)])]
    all_to_all x0 -> x1, waiting for transfers between devices: none -> 2.35 us  [exchange(): return lax.all_to_all(x, axis, 0, 0, tiled=True)]
  transfers between devices with their start and end apart: 0 -> 2, of which waited for: 0 -> 2; matrix products, arithmetic and copies ran while one was open for 0% -> 0% of each run, Pallas kernels for 0% -> 0%
where the time goes in v7:
time: 90.7 us; the launch traced here: 90.3 us
  blocking collectives  66.8 us (74%)
  starting transfers between devices  11 us (12%)
  waiting for transfers between devices  6.06 us (7%)
  Pallas kernels  5.79 us (6%)
    all_to_all x3, blocking collectives, exchange(): return lax.all_to_all(x, axis, 0, 0, tiled=True)  66.8 us
    all_to_all x1, starting transfers between devices, exchange(): return lax.all_to_all(x, axis, 0, 0, tiled=True)  7.76 us
    pallas_call x5, Pallas kernels, call(): pl.pallas_call(kernel, out_shape=out, in_specs=[pl.BlockSpec(memory_space...  5.79 us
    ppermute x1, waiting for transfers between devices, body(): other = lax.ppermute(keep, 'xl', [(0, 1), (1, 0)])  3.71 us
    ppermute x1, starting transfers between devices, body(): other = lax.ppermute(keep, 'xl', [(0, 1), (1, 0)])  3.29 us
    all_to_all x1, waiting for transfers between devices, exchange(): return lax.all_to_all(x, axis, 0, 0, tiled=True)  2.35 us
  transfers between devices with their start and end apart: 2, of which 2 were waited for; matrix products, arithmetic and copies ran while one was open for 0% of the time, Pallas kernels for 0%

profile of v7, /device:TPU:1, one launch (start us, length us, event | category | flops | bytes accessed | tf_op | source)
XLA Modules:
  0.0 90.3 jit_solution(18210675764981682638)
XLA Ops:
  0.6 2.1 %shard_map.50 = bf16[1088,128]{1,0:T(8,128)(2,1)S(1)} custom-call(s32[1,2048]{1,0:T(1,128)} %bitcast.12, bf16[64,2048]{1,0:T(8,128)(2,1)} %bitcast.11), custom_call_target="tpu_custom_call" | custom-call | tf_op jit(solution)/shard_map/pallas_call | solution.py:249
  2.7 27.4 %all_to_all.20 = bf16[32,17,2,128]{3,2,1,0:T(2,128)(2,1)S(1)} all-to-all(bf16[32,17,2,128]{3,2,1,0:T(2,128)(2,1)S(1)} %bitcast.8), channel_id=1, replica_groups=mesh['pair'=16,'core'=2,'y'=8,'xl'=2] {'pair','core'}, dimensions={0} | all-to-all | bytes 557056 | tf_op jit(solution)/shard_map/all_to_all | solution.py:265
  30.2 2.0 %shard_map.51 = (bf16[32,16,128]{2,1,0:T(8,128)(2,1)}, f32[32,768]{1,0:T(8,128)S(1)}, f32[8,768]{1,0:T(8,128)S(1)}) custom-call(s32[1,24]{1,0:T(1,128)} %bitcast.13, bf16[1088,128]{1,0:T(8,128)(2,1)S(1)} %bitcast.7), custom_call_target="tpu_custom_call" | custom-call | tf_op jit(solution)/shard_map/pallas_call | solution.py:249
  32.2 7.8 %all-to-all-start.1 = ((bf16[32,16,128]{2,1,0:T(8,128)(2,1)}), bf16[32,16,128]{2,1,0:T(8,128)(2,1)S(1)}, u32[]{:S(2)}, u32[]{:S(2)}) async-start(bf16[32,16,128]{2,1,0:T(8,128)(2,1)} %get-tuple-element.9), calls=%async_computation.1 | async-start | bytes 262144 | tf_op jit(solution)/shard_map/all_to_all | solution.py:265
  40.0 3.3 %collective-permute-start = (f32[32,768]{1,0:T(8,128)S(1)}, f32[32,768]{1,0:T(8,128)S(1)}, u32[]{:S(2)}, u32[]{:S(2)}) collective-permute-start(f32[32,768]{1,0:T(8,128)S(1)} %get-tuple-element.10.keep_ref), channel_id=1, source_target_pairs={{0,1},{1,0},{2,3},{3,2},{4,5},{5,4},{6,7},{7,6},{8,9},{9,8},{10,11... | collective-permute-start | bytes 294920 | tf_op jit(solution)/shard_map/ppermute | solution.py:294
  43.3 3.7 %collective-permute-done.other_ref = f32[32,768]{1,0:T(8,128)S(1)} collective-permute-done((f32[32,768]{1,0:T(8,128)S(1)}, f32[32,768]{1,0:T(8,128)S(1)}, u32[]{:S(2)}, u32[]{:S(2)}) %collective-permute-start) | collective-permute-done | bytes 98336 | tf_op jit(solution)/shard_map/ppermute | solution.py:294
  47.0 2.4 %all-to-all-done.1.in_ref = bf16[32,16,128]{2,1,0:T(8,128)(2,1)S(1)} async-done(((bf16[32,16,128]{2,1,0:T(8,128)(2,1)}), bf16[32,16,128]{2,1,0:T(8,128)(2,1)S(1)}, u32[]{:S(2)}, u32[]{:S(2)}) %all-to-all-start.1) | async-done | bytes 131104 | tf_op jit(solution)/shard_map/all_to_all | solution.py:265
  49.3 0.6 shard_map.52
  49.9 21.3 %all_to_all.21 = bf16[128,4,128]{2,1,0:T(4,128)(2,1)S(1)} all-to-all(bf16[128,4,128]{2,1,0:T(4,128)(2,1)S(1)} %bitcast.10), channel_id=1, replica_groups=mesh['pair'=16,'core'=2,'y'=8,'xl'=2] {'pair','y'}, dimensions={0} | all-to-all | bytes 262144 | tf_op jit(solution)/shard_map/all_to_all | solution.py:265
  71.1 0.2 shard_map.53
  71.3 18.1 %all_to_all.22.in_ref = bf16[32,32,128]{2,1,0:T(8,128)(2,1)S(1)} all-to-all(bf16[32,32,128]{2,1,0:T(8,128)(2,1)S(1)} %shard_map.53), channel_id=1, replica_groups=mesh['pair'=16,'core'=2,'y'=8,'xl'=2] {'pair','core'}, dimensions={0} | all-to-all | bytes 524288 | tf_op jit(solution)/shard_map/all_to_all | solution.py:265
  89.4 0.9 %shard_map.54 = (bf16[128,1024]{1,0:T(8,128)(2,1)}, bf16[24,1024]{1,0:T(8,128)(2,1)}) custom-call(bf16[32,32,128]{2,1,0:T(8,128)(2,1)S(1)} %all_to_all.22.in_ref, bf16[24,1024]{1,0:T(8,128)(2,1)S(1)} %get-tuple-element.13.level2_ref), custom_call_target="tpu_custom_call" | custom-call | tf_op jit(solution)/shard_map/pallas_call | solution.py:249
Async XLA Ops:
  32.2 17.1 %all-to-all-start.1 = ((bf16[32,16,128]{2,1,0:T(8,128)(2,1)}), bf16[32,16,128]{2,1,0:T(8,128)(2,1)S(1)}, u32[]{:S(2)}, u32[]{:S(2)}) async-start(bf16[32,16,128]{2,1,0:T(8,128)(2,1)} %get-tuple-element.9), calls=%async_computation.1 | async-start | bytes 262144 | tf_op jit(solution)/shard_map/all_to_all | solution.py:265
  40.0 7.0 %collective-permute-start = (f32[32,768]{1,0:T(8,128)S(1)}, f32[32,768]{1,0:T(8,128)S(1)}, u32[]{:S(2)}, u32[]{:S(2)}) collective-permute-start(f32[32,768]{1,0:T(8,128)S(1)} %get-tuple-element.10.keep_ref), channel_id=1, source_target_pairs={{0,1},{1,0},{2,3},{3,2},{4,5},{5,4},{6,7},{7,6},{8,9},{9,8},{10,11... | collective-permute-start | bytes 294920 | tf_op jit(solution)/shard_map/ppermute | solution.py:294

commit v8 on v7

--- a/solution.py
+++ b/solution.py
@@ -80,9 +80,10 @@
 
     line = iota((N_DP, PTS), 0)
     digit = jnp.where((line & 1) == 0, local >> 3, local & 7).astype(f32)
-    digit = jnp.where((line >> 1) == (group >> 1), digit, 0.0).astype(bf16)
-    place = lax.axis_index("pair") * 2 + lax.axis_index("core")
-    slot = (group & 1) * 4 + (r1 & 3)
+    pair = ((group >> 2) << 1) | (group & 1)
+    digit = jnp.where((line >> 1) == pair, digit, 0.0).astype(bf16)
+    place = lax.axis_index("z") * 4 + lax.axis_index("xh") * 2 + lax.axis_index("core")
+    slot = ((group >> 1) & 1) * 4 + (r1 & 3)
     spot = (16 * (place + slot) + (r1 >> 2) * 8 + r2) & 127
 
     fetch_points.wait()
@@ -94,11 +95,12 @@
     moved = dot_nt(key, split)
     tags = dot_nt(digit, rows_of(spot.astype(f32), 128))
     for d in range(N_DP):
-        pair, half = d >> 1, d & 1
+        first, half = d & ~2, (d >> 1) & 1
+        pair = (d >> 2) * 2 + (d & 1)
         for own in range(2):
             for h in range(2):
                 at = STRIDE * d + 16 * own + 8 * h
-                line, lane = 8 * (2 * pair + own), 256 * half + 128 * h
+                line, lane = 8 * (first + 2 * own), 256 * half + 128 * h
                 rows_ref[at : at + 8, :] = moved[line : line + 8, lane : lane + 128]
         rows_ref[STRIDE * d + 32 : STRIDE * d + 34, :] = tags[2 * pair : 2 * pair + 2]
     out_ref[...] = rows_ref[...].astype(bf16)
@@ -213,7 +215,7 @@
     swapped = pltpu.roll(total, 4, 1)
     swapped = jnp.where(lower == 0, pltpu.roll(swapped, 32, 2), pltpu.roll(swapped, 96, 2))
     out = jnp.where(odd == lower, total, swapped)
-    out = jnp.where(lax.axis_index("core") == 1, pltpu.roll(out, 32, 2), out)
+    out = jnp.where(lax.axis_index("xh") == 1, pltpu.roll(out, 32, 2), out)
     out_ref[...] = jnp.broadcast_to(out.reshape(32, 128).astype(bf16)[None], (N_DP, 32, 128))
 
 
@@ -221,12 +223,13 @@
     stores = [pltpu.make_async_copy(level2_ref, level2_hbm, sems.at[2])]
     stores[0].start()
     band = iota((N_MP, 8, 128), 2) >> 5
+    places = [(p >> 1) * 4 + (p & 1) for p in range(N_DP // 2)]
     tiles = []
     square = jnp.zeros((N_MP, 8, 128), f32)
     for t in range(4):
         block = pl.ds(8 * t, 8)
-        first = jnp.concatenate([in_ref[2 * p : 2 * p + 1, block, :] for p in range(N_MP)], axis=0).astype(f32)
-        second = jnp.concatenate([in_ref[2 * p + 1 : 2 * p + 2, block, :] for p in range(N_MP)], axis=0).astype(f32)
+        first = jnp.concatenate([in_ref[n : n + 1, block, :] for n in places], axis=0).astype(f32)
+        second = jnp.concatenate([in_ref[n + 2 : n + 3, block, :] for n in places], axis=0).astype(f32)
         even = (band & 1) == 0
         tiles.append(jnp.where(even, first, second))
         tiles.append(pltpu.roll(jnp.where(even, second, first), 96, 2))
@@ -278,7 +281,7 @@
             pltpu.SemaphoreType.DMA((2,)),
         ),
     )
-    got = exchange(sent.reshape(N_DP, STRIDE // 2, 2, 128), ("pair", "core")).reshape(rows, 128)
+    got = exchange(sent.reshape(N_DP, STRIDE // 2, 2, 128), ("z", "xh", "core")).reshape(rows, 128)
     sums, keep, counts = call(
         sum_kernel,
         (shape((2 * N_MP, 16, 128), bf16), shape((32, 2 * GROUP), f32), shape((8, 2 * GROUP), f32)),
@@ -296,18 +299,18 @@
     level2, partial = call(
         unit_kernel,
         (shape((ROWS, D), bf16), shape((4 * peers, 128), bf16)),
-        exchange(sums, ("core", "y", "xl")),
+        exchange(sums, ("xh", "y", "xl")),
         keep,
         other,
         counts,
         spaces=(pltpu.VMEM, pltpu.VMEM),
     )
-    parts = exchange(partial.reshape(peers, 4, 128), ("pair", "y")).reshape(4 * peers, 128)
+    parts = exchange(partial.reshape(peers, 4, 128), ("z", "core", "y")).reshape(4 * peers, 128)
     parents = call(spread_kernel, shape((N_DP, 32, 128), bf16), parts)
     level3, level2 = call(
         finish_kernel,
         (shape((K3_MP, D), bf16), shape((ROWS, D), bf16)),
-        exchange(parents, ("pair", "core")),
+        exchange(parents, ("z", "xh", "core")),
         level2,
         scratch=(pltpu.VMEM((K3_MP, D), bf16), pltpu.SemaphoreType.DMA((3,))),
         spaces=(pltpu.HBM, pltpu.HBM),
@@ -316,8 +319,8 @@
 
 
 def solution(mesh):
-    split = Mesh(mesh.devices.reshape(N_DP // 2, 2, N_MP // 2, 2), ("pair", "core", "y", "xl"))
-    dp, mp = ("pair", "core"), ("y", "xl")
+    split = Mesh(mesh.devices.reshape(N_DP // 4, 2, 2, N_MP // 2, 2), ("z", "xh", "core", "y", "xl"))
+    dp, mp = ("z", "xh", "core"), ("y", "xl")
     placed = (P(dp, mp), P(dp, None), P((*dp, *mp), None))
     return jax.shard_map(
         body,

time: 90.7 us -> 90.1 us (level)
  blocking collectives: 66.8 us -> 65.1 us
    all_to_all x3, blocking collectives: 66.8 us -> 65.1 us  [exchange(): return lax.all_to_all(x, axis, 0, 0, tiled=True)]
    all_to_all x1, waiting for transfers between devices: 2.35 us -> 3.87 us  [exchange(): return lax.all_to_all(x, axis, 0, 0, tiled=True)]
where the time goes in v8:
time: 90.1 us; the launch traced here: 89.7 us
  blocking collectives  65.1 us (72%)
  starting transfers between devices  11.3 us (13%)
  waiting for transfers between devices  6.86 us (8%)
  Pallas kernels  5.79 us (6%)
    all_to_all x3, blocking collectives, exchange(): return lax.all_to_all(x, axis, 0, 0, tiled=True)  65.1 us
    all_to_all x1, starting transfers between devices, exchange(): return lax.all_to_all(x, axis, 0, 0, tiled=True)  8.15 us
    pallas_call x5, Pallas kernels, call(): pl.pallas_call(kernel, out_shape=out, in_specs=[pl.BlockSpec(memory_space...  5.79 us
    all_to_all x1, waiting for transfers between devices, exchange(): return lax.all_to_all(x, axis, 0, 0, tiled=True)  3.87 us
    ppermute x1, starting transfers between devices, body(): other = lax.ppermute(keep, 'xl', [(0, 1), (1, 0)])  3.14 us
    ppermute x1, waiting for transfers between devices, body(): other = lax.ppermute(keep, 'xl', [(0, 1), (1, 0)])  2.99 us
  transfers between devices with their start and end apart: 2, of which 2 were waited for; matrix products, arithmetic and copies ran while one was open for 0% of the time, Pallas kernels for 0%

profile of v8, /device:TPU:1, one launch (start us, length us, event | category | flops | bytes accessed | tf_op | source)
XLA Modules:
  0.0 89.7 jit_solution(648006975875244588)
XLA Ops:
  0.6 2.1 %shard_map.50 = bf16[1088,128]{1,0:T(8,128)(2,1)S(1)} custom-call(s32[1,2048]{1,0:T(1,128)} %bitcast.12, bf16[64,2048]{1,0:T(8,128)(2,1)} %bitcast.11), custom_call_target="tpu_custom_call" | custom-call | tf_op jit(solution)/shard_map/pallas_call | solution.py:252
  2.7 27.4 %all_to_all.20 = bf16[32,17,2,128]{3,2,1,0:T(2,128)(2,1)S(1)} all-to-all(bf16[32,17,2,128]{3,2,1,0:T(2,128)(2,1)S(1)} %bitcast.8), channel_id=1, replica_groups=mesh['z'=8,'xh'=2,'core'=2,'y'=8,'xl'=2] {'z','xh','core'}, dimensions={0} | all-to-all | bytes 557056 | tf_op jit(solution)/shard_map/all_to_all | solution.py:268
  30.2 2.0 %shard_map.51 = (bf16[32,16,128]{2,1,0:T(8,128)(2,1)}, f32[32,768]{1,0:T(8,128)S(1)}, f32[8,768]{1,0:T(8,128)S(1)}) custom-call(s32[1,24]{1,0:T(1,128)} %bitcast.13, bf16[1088,128]{1,0:T(8,128)(2,1)S(1)} %bitcast.7), custom_call_target="tpu_custom_call" | custom-call | tf_op jit(solution)/shard_map/pallas_call | solution.py:252
  32.2 8.2 %all-to-all-start.1 = ((bf16[32,16,128]{2,1,0:T(8,128)(2,1)}), bf16[32,16,128]{2,1,0:T(8,128)(2,1)S(1)}, u32[]{:S(2)}, u32[]{:S(2)}) async-start(bf16[32,16,128]{2,1,0:T(8,128)(2,1)} %get-tuple-element.9), calls=%async_computation.1 | async-start | bytes 262144 | tf_op jit(solution)/shard_map/all_to_all | solution.py:268
  40.4 3.1 %collective-permute-start = (f32[32,768]{1,0:T(8,128)S(1)}, f32[32,768]{1,0:T(8,128)S(1)}, u32[]{:S(2)}, u32[]{:S(2)}) collective-permute-start(f32[32,768]{1,0:T(8,128)S(1)} %get-tuple-element.10.keep_ref), channel_id=1, source_target_pairs={{0,1},{1,0},{2,3},{3,2},{4,5},{5,4},{6,7},{7,6},{8,9},{9,8},{10,11... | collective-permute-start | bytes 294920 | tf_op jit(solution)/shard_map/ppermute | solution.py:297
  43.5 3.0 %collective-permute-done.other_ref = f32[32,768]{1,0:T(8,128)S(1)} collective-permute-done((f32[32,768]{1,0:T(8,128)S(1)}, f32[32,768]{1,0:T(8,128)S(1)}, u32[]{:S(2)}, u32[]{:S(2)}) %collective-permute-start) | collective-permute-done | bytes 98336 | tf_op jit(solution)/shard_map/ppermute | solution.py:297
  46.5 3.9 %all-to-all-done.1.in_ref = bf16[32,16,128]{2,1,0:T(8,128)(2,1)S(1)} async-done(((bf16[32,16,128]{2,1,0:T(8,128)(2,1)}), bf16[32,16,128]{2,1,0:T(8,128)(2,1)S(1)}, u32[]{:S(2)}, u32[]{:S(2)}) %all-to-all-start.1) | async-done | bytes 131104 | tf_op jit(solution)/shard_map/all_to_all | solution.py:268
  50.4 0.6 shard_map.52
  50.9 19.8 %all_to_all.21 = bf16[128,4,128]{2,1,0:T(4,128)(2,1)S(1)} all-to-all(bf16[128,4,128]{2,1,0:T(4,128)(2,1)S(1)} %bitcast.10), channel_id=1, replica_groups=mesh['z'=8,'xh'=2,'core'=2,'y'=8,'xl'=2] {'z','core','y'}, dimensions={0} | all-to-all | bytes 262144 | tf_op jit(solution)/shard_map/all_to_all | solution.py:268
  70.7 0.2 shard_map.53
  70.9 17.9 %all_to_all.22.in_ref = bf16[32,32,128]{2,1,0:T(8,128)(2,1)S(1)} all-to-all(bf16[32,32,128]{2,1,0:T(8,128)(2,1)S(1)} %shard_map.53), channel_id=1, replica_groups=mesh['z'=8,'xh'=2,'core'=2,'y'=8,'xl'=2] {'z','xh','core'}, dimensions={0} | all-to-all | bytes 524288 | tf_op jit(solution)/shard_map/all_to_all | solution.py:268
  88.8 0.9 %shard_map.54 = (bf16[128,1024]{1,0:T(8,128)(2,1)}, bf16[24,1024]{1,0:T(8,128)(2,1)}) custom-call(bf16[32,32,128]{2,1,0:T(8,128)(2,1)S(1)} %all_to_all.22.in_ref, bf16[24,1024]{1,0:T(8,128)(2,1)S(1)} %get-tuple-element.13.level2_ref), custom_call_target="tpu_custom_call" | custom-call | tf_op jit(solution)/shard_map/pallas_call | solution.py:252
Async XLA Ops:
  32.2 18.2 %all-to-all-start.1 = ((bf16[32,16,128]{2,1,0:T(8,128)(2,1)}), bf16[32,16,128]{2,1,0:T(8,128)(2,1)S(1)}, u32[]{:S(2)}, u32[]{:S(2)}) async-start(bf16[32,16,128]{2,1,0:T(8,128)(2,1)} %get-tuple-element.9), calls=%async_computation.1 | async-start | bytes 262144 | tf_op jit(solution)/shard_map/all_to_all | solution.py:268
  40.4 6.1 %collective-permute-start = (f32[32,768]{1,0:T(8,128)S(1)}, f32[32,768]{1,0:T(8,128)S(1)}, u32[]{:S(2)}, u32[]{:S(2)}) collective-permute-start(f32[32,768]{1,0:T(8,128)S(1)} %get-tuple-element.10.keep_ref), channel_id=1, source_target_pairs={{0,1},{1,0},{2,3},{3,2},{4,5},{5,4},{6,7},{7,6},{8,9},{9,8},{10,11... | collective-permute-start | bytes 294920 | tf_op jit(solution)/shard_map/ppermute | solution.py:297

commit v9 on v8

--- a/solution.py
+++ b/solution.py
@@ -154,7 +154,7 @@
     out_ref[:, 8:16, :] = jnp.broadcast_to(tail[None], (2 * N_MP, 8, 128))
 
 
-def unit_kernel(in_ref, keep_ref, other_ref, count_ref, level2_ref, out_ref):
+def unit_kernel(in_ref, keep_ref, count_ref, level2_ref, out_ref):
     band = iota((8, 128), 1) >> 5
     rows = ([], [], [])
     for c in range(N_MP // 2):
@@ -186,23 +186,12 @@
         mine = ((place >> 3) * 171) >> 9 == iota((2 * N_MP, 128), 0)
         parent.append(jnp.sum(jnp.where(mine, named, 0.0), axis=0, keepdims=True))
     parent = jnp.concatenate(parent, axis=1).astype(i32)
-    side = lax.axis_index("xl")
-    line = (((parent >> 3) & 15) * 8 + (parent >> 8)) * 4 + (parent & 3)
-    line = jnp.where(((parent >> 7) & 1) == side, line, -1)
+    line = (((parent >> 3) & 15) * 8 + (parent >> 8)) * 4 + ((parent >> 7) & 1) * 2 + (parent & 1)
     key = rows_of(line.astype(f32), N_DP * N_MP)
 
-    factor = count_ref[0:1, :]
-    own = (keep_ref[...] * scale).astype(bf16).astype(f32) * factor
-    other = (other_ref[...] * scale).astype(bf16).astype(f32) * factor
-    part = (parent >> 2) & 1
-    both = jnp.concatenate(
-        [
-            jnp.where(part == s, block, 0.0)
-            for block in (jnp.where(side == 0, own, other), jnp.where(side == 0, other, own))
-            for s in range(2)
-        ],
-        axis=0,
-    )
+    weighted = (keep_ref[...] * scale).astype(bf16).astype(f32) * count_ref[0:1, :]
+    part = (parent >> 1) & 3
+    both = jnp.concatenate([jnp.where(part == s, weighted, 0.0) for s in range(4)], axis=0)
     high = both.astype(bf16)
     low = (both - high.astype(f32)).astype(bf16)
     total = dot_nt(key, jnp.concatenate([high, low], axis=0))
@@ -211,29 +200,48 @@
 
 def spread_kernel(in_ref, out_ref):
     total = jnp.sum(in_ref[...].astype(f32).reshape(N_DP // 2, 32, 128), axis=0).reshape(4, 8, 128)
-    odd, lower = (iota((4, 8, 128), 2) >> 5) & 1, iota((4, 8, 128), 1) >> 2
-    swapped = pltpu.roll(total, 4, 1)
-    swapped = jnp.where(lower == 0, pltpu.roll(swapped, 32, 2), pltpu.roll(swapped, 96, 2))
-    out = jnp.where(odd == lower, total, swapped)
-    out = jnp.where(lax.axis_index("xh") == 1, pltpu.roll(out, 32, 2), out)
-    out_ref[...] = jnp.broadcast_to(out.reshape(32, 128).astype(bf16)[None], (N_DP, 32, 128))
+    band, part = iota((2, 8, 128), 2) >> 5, iota((2, 8, 128), 1) >> 1
+    even = jnp.concatenate([total[0:1], total[2:3]], axis=0)
+    odd = jnp.concatenate([total[1:2], total[3:4]], axis=0)
+    pieces = []
+    for xl in range(2):
+        out = jnp.zeros((2, 8, 128), f32)
+        for y in range(4):
+            for s in range(4):
+                piece = odd if y >> 1 else even
+                across, down = (32 * (y - s)) % 128, (2 * s - 4 * (y & 1) - 2 * xl) % 8
+                piece = pltpu.roll(piece, across, 2) if across else piece
+                piece = pltpu.roll(piece, down, 1) if down else piece
+                out = jnp.where((band == y) & (part == s), piece, out)
+        pieces.append(out)
+    out = jnp.concatenate(pieces, axis=0)
+    place = 2 * lax.axis_index("xl") + lax.axis_index("xh")
+    turned = out
+    for n in range(1, 4):
+        turned = jnp.where(place == n, pltpu.roll(out, 32 * n, 2), turned)
+    out_ref[...] = jnp.broadcast_to(turned.reshape(32, 128).astype(bf16)[None], (N_DP, 32, 128))
 
 
 def finish_kernel(in_ref, level2_ref, out_hbm, level2_hbm, out_ref, sems):
     stores = [pltpu.make_async_copy(level2_ref, level2_hbm, sems.at[2])]
     stores[0].start()
-    band = iota((N_MP, 8, 128), 2) >> 5
+    band = iota((N_DP // 2, 8, 128), 2) >> 5
     places = [(p >> 1) * 4 + (p & 1) for p in range(N_DP // 2)]
     tiles = []
-    square = jnp.zeros((N_MP, 8, 128), f32)
-    for t in range(4):
+    square = jnp.zeros((N_DP // 2, 8, 128), f32)
+    for t in range(2):
         block = pl.ds(8 * t, 8)
-        first = jnp.concatenate([in_ref[n : n + 1, block, :] for n in places], axis=0).astype(f32)
-        second = jnp.concatenate([in_ref[n + 2 : n + 3, block, :] for n in places], axis=0).astype(f32)
-        even = (band & 1) == 0
-        tiles.append(jnp.where(even, first, second))
-        tiles.append(pltpu.roll(jnp.where(even, second, first), 96, 2))
-        square = square + tiles[-1] * tiles[-1] + tiles[-2] * tiles[-2]
+        parts = []
+        for n in range(4):
+            source = [2 * (place + 2 * (n & 1)) + (n >> 1) for place in places]
+            parts.append(jnp.concatenate([in_ref[m : m + 1, block, :] for m in source], axis=0).astype(f32))
+        for y in range(4):
+            tile = parts[0]
+            for n in range(1, 4):
+                tile = jnp.where(band == (y + n) % 4, parts[n], tile)
+            tile = pltpu.roll(tile, 128 - 32 * y, 2) if y else tile
+            tiles.append(tile)
+            square = square + tile * tile
     scale = lax.rsqrt(jnp.sum(square, axis=2, keepdims=True) * (1.0 / D) + EPS)
     for n in range(2):
         block = pl.ds(64 * n, 64)
@@ -294,14 +302,12 @@
         ),
         spaces=(pltpu.VMEM,) * 3,
     )
-    other = lax.ppermute(keep, "xl", [(0, 1), (1, 0)])
     peers = N_DP // 2 * N_MP // 2
     level2, partial = call(
         unit_kernel,
         (shape((ROWS, D), bf16), shape((4 * peers, 128), bf16)),
         exchange(sums, ("xh", "y", "xl")),
         keep,
-        other,
         counts,
         spaces=(pltpu.VMEM, pltpu.VMEM),
     )
@@ -310,7 +316,7 @@
     level3, level2 = call(
         finish_kernel,
         (shape((K3_MP, D), bf16), shape((ROWS, D), bf16)),
-        exchange(parents, ("z", "xh", "core")),
+        exchange(parents.reshape(2 * N_DP, 16, 128), ("z", "xh", "core", "xl")),
         level2,
         scratch=(pltpu.VMEM((K3_MP, D), bf16), pltpu.SemaphoreType.DMA((3,))),
         spaces=(pltpu.HBM, pltpu.HBM),

time: 90.1 us -> 89.1 us (0.989)
  blocking collectives: 65.1 us -> 82.9 us
  starting transfers between devices: 11.3 us -> 0 us
  waiting for transfers between devices: 6.86 us -> 0 us
    all_to_all x3 -> x4, blocking collectives: 65.1 us -> 82.9 us  [exchange(): return lax.all_to_all(x, axis, 0, 0, tiled=True)]
    all_to_all x1 -> x0, starting transfers between devices: 8.15 us -> none  [exchange(): return lax.all_to_all(x, axis, 0, 0, tiled=True)]
    all_to_all x1 -> x0, waiting for transfers between devices: 3.87 us -> none  [exchange(): return lax.all_to_all(x, axis, 0, 0, tiled=True)]
    ppermute x1 -> x0, starting transfers between devices: 3.14 us -> none  [body(): other = lax.ppermute(keep, 'xl', [(0, 1), (1, 0)])]
    ppermute x1 -> x0, waiting for transfers between devices: 2.99 us -> none  [body(): other = lax.ppermute(keep, 'xl', [(0, 1), (1, 0)])]
  transfers between devices with their start and end apart: 2 -> 0, of which waited for: 2 -> 0; matrix products, arithmetic and copies ran while one was open for 0% -> 0% of each run, Pallas kernels for 0% -> 0%
where the time goes in v9:
time: 89.1 us; the launch traced here: 88.8 us
  blocking collectives  82.9 us (93%)
  Pallas kernels  5.17 us (6%)
    all_to_all x4, blocking collectives, exchange(): return lax.all_to_all(x, axis, 0, 0, tiled=True)  82.9 us
    pallas_call x5, Pallas kernels, call(): pl.pallas_call(kernel, out_shape=out, in_specs=[pl.BlockSpec(memory_space...  5.17 us

profile of v9, /device:TPU:1, one launch (start us, length us, event | category | flops | bytes accessed | tf_op | source)
XLA Modules:
  0.0 88.8 jit_solution(3143275937163963339)
XLA Ops:
  0.6 2.1 %shard_map.50 = bf16[1088,128]{1,0:T(8,128)(2,1)S(1)} custom-call(s32[1,2048]{1,0:T(1,128)} %bitcast.14, bf16[64,2048]{1,0:T(8,128)(2,1)} %bitcast.13), custom_call_target="tpu_custom_call" | custom-call | tf_op jit(solution)/shard_map/pallas_call | solution.py:260
  2.7 27.4 %all_to_all.20 = bf16[32,17,2,128]{3,2,1,0:T(2,128)(2,1)S(1)} all-to-all(bf16[32,17,2,128]{3,2,1,0:T(2,128)(2,1)S(1)} %bitcast.9), channel_id=1, replica_groups=mesh['z'=8,'xh'=2,'core'=2,'y'=8,'xl'=2] {'z','xh','core'}, dimensions={0} | all-to-all | bytes 557056 | tf_op jit(solution)/shard_map/all_to_all | solution.py:276
  30.2 1.4 %shard_map.51 = (bf16[32,16,128]{2,1,0:T(8,128)(2,1)S(1)}, f32[32,768]{1,0:T(8,128)S(1)}, f32[8,768]{1,0:T(8,128)S(1)}) custom-call(s32[1,24]{1,0:T(1,128)} %bitcast.15, bf16[1088,128]{1,0:T(8,128)(2,1)S(1)} %bitcast.8), custom_call_target="tpu_custom_call" | custom-call | tf_op jit(solution)/shard_map/pallas_call | solution.py:260
  31.6 18.0 %all_to_all.21.in_ref = bf16[32,16,128]{2,1,0:T(8,128)(2,1)S(1)} all-to-all(bf16[32,16,128]{2,1,0:T(8,128)(2,1)S(1)} %get-tuple-element.9), channel_id=1, replica_groups=mesh['z'=8,'xh'=2,'core'=2,'y'=8,'xl'=2] {'xh','y','xl'}, dimensions={0} | all-to-all | bytes 262144 | tf_op jit(solution)/shard_map/all_to_all | solution.py:276
  49.5 0.5 shard_map.52
  50.1 19.8 %all_to_all.22 = bf16[128,4,128]{2,1,0:T(4,128)(2,1)S(1)} all-to-all(bf16[128,4,128]{2,1,0:T(4,128)(2,1)S(1)} %bitcast.12), channel_id=1, replica_groups=mesh['z'=8,'xh'=2,'core'=2,'y'=8,'xl'=2] {'z','core','y'}, dimensions={0} | all-to-all | bytes 262144 | tf_op jit(solution)/shard_map/all_to_all | solution.py:276
  69.9 0.2 shard_map.53
  70.1 17.8 %all_to_all.23.in_ref = bf16[64,16,128]{2,1,0:T(8,128)(2,1)S(1)} all-to-all(bf16[64,16,128]{2,1,0:T(8,128)(2,1)S(1)} %bitcast.10), channel_id=1, replica_groups=mesh['z'=8,'xh'=2,'core'=2,'y'=8,'xl'=2] {'z','xh','core','xl'}, dimensions={0} | all-to-all | bytes 524288 | tf_op jit(solution)/shard_map/all_to_all | solution.py:276
  87.8 1.0 %shard_map.54 = (bf16[128,1024]{1,0:T(8,128)(2,1)}, bf16[24,1024]{1,0:T(8,128)(2,1)}) custom-call(bf16[64,16,128]{2,1,0:T(8,128)(2,1)S(1)} %all_to_all.23.in_ref, bf16[24,1024]{1,0:T(8,128)(2,1)S(1)} %get-tuple-element.13.level2_ref), custom_call_target="tpu_custom_call" | custom-call | tf_op jit(solution)/shard_map/pallas_call | solution.py:260

commit v10 on v9

--- a/solution.py
+++ b/solution.py
@@ -148,9 +148,8 @@
     parent = jnp.concatenate([parent >> 3, parent & 7], axis=0).astype(f32)
     parent = jnp.concatenate([parent, jnp.zeros((2, 128 - ROWS), f32)], axis=1)
     tail = jnp.concatenate(squares + [parent], axis=0).astype(bf16)
-    for own in range(2):
-        block = slice(N_MP * own, N_MP * (own + 1))
-        out_ref[block, 0:8, :] = wides[own]
+    wides = [wide.reshape(N_MP // 2, 1, 2, 8, 128) for wide in wides]
+    out_ref[:, 0:8, :] = jnp.concatenate(wides, axis=1).reshape(2 * N_MP, 8, 128)
     out_ref[:, 8:16, :] = jnp.broadcast_to(tail[None], (2 * N_MP, 8, 128))
 
 
@@ -160,7 +159,7 @@
     for c in range(N_MP // 2):
         parts = []
         for b in range(4):
-            source = N_MP * (b & 1) + 2 * c + (b >> 1)
+            source = 4 * c + 2 * (b & 1) + (b >> 1)
             parts.append(in_ref[source, 0:8, :].astype(f32))
         for g in range(3):
             line = None
@@ -177,8 +176,13 @@
     squares = jnp.concatenate([squares[c : c + 1] for c in range(6)], axis=1)
     scale = lax.rsqrt(squares * (1.0 / D) + EPS)
     named = 8.0 * tails[:, 6:7] + tails[:, 7:8]
+    order = [4 * (n % N_MP >> 1) + 2 * (n // N_MP) + (n & 1) for n in range(2 * N_MP)]
     named = jnp.concatenate(
-        [pltpu.roll(named[n], (ROWS * n) % 128, 1) if n % N_MP else named[n] for n in range(2 * N_MP)], axis=0
+        [
+            pltpu.roll(named[m], (ROWS * n) % 128, 1) if n % N_MP else named[m]
+            for n, m in enumerate(order)
+        ],
+        axis=0,
     )
     parent = []
     for c in range(6):
@@ -186,7 +190,8 @@
         mine = ((place >> 3) * 171) >> 9 == iota((2 * N_MP, 128), 0)
         parent.append(jnp.sum(jnp.where(mine, named, 0.0), axis=0, keepdims=True))
     parent = jnp.concatenate(parent, axis=1).astype(i32)
-    line = (((parent >> 3) & 15) * 8 + (parent >> 8)) * 4 + ((parent >> 7) & 1) * 2 + (parent & 1)
+    device = (parent >> 8) * 16 + ((parent >> 3) & 1) * 8 + ((parent >> 4) & 7)
+    line = device * 4 + ((parent >> 7) & 1) * 2 + (parent & 1)
     key = rows_of(line.astype(f32), N_DP * N_MP)
 
     weighted = (keep_ref[...] * scale).astype(bf16).astype(f32) * count_ref[0:1, :]
@@ -199,7 +204,10 @@
 
 
 def spread_kernel(in_ref, out_ref):
-    total = jnp.sum(in_ref[...].astype(f32).reshape(N_DP // 2, 32, 128), axis=0).reshape(4, 8, 128)
+    total = jnp.sum(in_ref[...].astype(f32).reshape(8, 8, 8, 128), axis=1)
+    total = total + pltpu.roll(total, 4, 1)
+    total = total.reshape(4, 2, 8, 128)
+    total = jnp.where(iota((4, 8, 128), 1) < 4, total[:, 0], total[:, 1])
     band, part = iota((2, 8, 128), 2) >> 5, iota((2, 8, 128), 1) >> 1
     even = jnp.concatenate([total[0:1], total[2:3]], axis=0)
     odd = jnp.concatenate([total[1:2], total[3:4]], axis=0)
@@ -306,12 +314,12 @@
     level2, partial = call(
         unit_kernel,
         (shape((ROWS, D), bf16), shape((4 * peers, 128), bf16)),
-        exchange(sums, ("xh", "y", "xl")),
+        exchange(sums, ("y", "xh", "xl")),
         keep,
         counts,
         spaces=(pltpu.VMEM, pltpu.VMEM),
     )
-    parts = exchange(partial.reshape(peers, 4, 128), ("z", "core", "y")).reshape(4 * peers, 128)
+    parts = exchange(partial.reshape(peers, 4, 128), ("y", "core", "z")).reshape(4 * peers, 128)
     parents = call(spread_kernel, shape((N_DP, 32, 128), bf16), parts)
     level3, level2 = call(
         finish_kernel,

time: 89.1 us -> 88.8 us (level)
  no operation moved by 1% of the time
where the time goes in v10:
time: 88.8 us; the launch traced here: 88.5 us
  blocking collectives  82.7 us (93%)
  Pallas kernels  5.17 us (6%)
    all_to_all x4, blocking collectives, exchange(): return lax.all_to_all(x, axis, 0, 0, tiled=True)  82.7 us
    pallas_call x5, Pallas kernels, call(): pl.pallas_call(kernel, out_shape=out, in_specs=[pl.BlockSpec(memory_space...  5.17 us

profile of v10, /device:TPU:1, one launch (start us, length us, event | category | flops | bytes accessed | tf_op | source)
XLA Modules:
  0.0 88.5 jit_solution(14589987860681153641)
XLA Ops:
  0.6 2.1 %shard_map.50 = bf16[1088,128]{1,0:T(8,128)(2,1)S(1)} custom-call(s32[1,2048]{1,0:T(1,128)} %bitcast.14, bf16[64,2048]{1,0:T(8,128)(2,1)} %bitcast.13), custom_call_target="tpu_custom_call" | custom-call | tf_op jit(solution)/shard_map/pallas_call | solution.py:268
  2.7 27.4 %all_to_all.20 = bf16[32,17,2,128]{3,2,1,0:T(2,128)(2,1)S(1)} all-to-all(bf16[32,17,2,128]{3,2,1,0:T(2,128)(2,1)S(1)} %bitcast.9), channel_id=1, replica_groups=mesh['z'=8,'xh'=2,'core'=2,'y'=8,'xl'=2] {'z','xh','core'}, dimensions={0} | all-to-all | bytes 557056 | tf_op jit(solution)/shard_map/all_to_all | solution.py:284
  30.2 1.4 %shard_map.51 = (bf16[32,16,128]{2,1,0:T(8,128)(2,1)S(1)}, f32[32,768]{1,0:T(8,128)S(1)}, f32[8,768]{1,0:T(8,128)S(1)}) custom-call(s32[1,24]{1,0:T(1,128)} %bitcast.15, bf16[1088,128]{1,0:T(8,128)(2,1)S(1)} %bitcast.8), custom_call_target="tpu_custom_call" | custom-call | tf_op jit(solution)/shard_map/pallas_call | solution.py:268
  31.6 17.3 %all_to_all.21.in_ref = bf16[32,16,128]{2,1,0:T(8,128)(2,1)S(1)} all-to-all(bf16[32,16,128]{2,1,0:T(8,128)(2,1)S(1)} %get-tuple-element.9), channel_id=1, replica_groups=mesh['z'=8,'xh'=2,'core'=2,'y'=8,'xl'=2] {'y','xh','xl'}, dimensions={0} | all-to-all | bytes 262144 | tf_op jit(solution)/shard_map/all_to_all | solution.py:284
  48.8 0.5 shard_map.52
  49.4 19.9 %all_to_all.22 = bf16[128,4,128]{2,1,0:T(4,128)(2,1)S(1)} all-to-all(bf16[128,4,128]{2,1,0:T(4,128)(2,1)S(1)} %bitcast.12), channel_id=1, replica_groups=mesh['z'=8,'xh'=2,'core'=2,'y'=8,'xl'=2] {'y','core','z'}, dimensions={0} | all-to-all | bytes 262144 | tf_op jit(solution)/shard_map/all_to_all | solution.py:284
  69.3 0.2 shard_map.53
  69.5 18.1 %all_to_all.23.in_ref = bf16[64,16,128]{2,1,0:T(8,128)(2,1)S(1)} all-to-all(bf16[64,16,128]{2,1,0:T(8,128)(2,1)S(1)} %bitcast.10), channel_id=1, replica_groups=mesh['z'=8,'xh'=2,'core'=2,'y'=8,'xl'=2] {'z','xh','core','xl'}, dimensions={0} | all-to-all | bytes 524288 | tf_op jit(solution)/shard_map/all_to_all | solution.py:284
  87.6 1.0 %shard_map.54 = (bf16[128,1024]{1,0:T(8,128)(2,1)}, bf16[24,1024]{1,0:T(8,128)(2,1)}) custom-call(bf16[64,16,128]{2,1,0:T(8,128)(2,1)S(1)} %all_to_all.23.in_ref, bf16[24,1024]{1,0:T(8,128)(2,1)S(1)} %get-tuple-element.13.level2_ref), custom_call_target="tpu_custom_call" | custom-call | tf_op jit(solution)/shard_map/pallas_call | solution.py:268

commit v11 on v10

--- a/solution.py
+++ b/solution.py
@@ -190,8 +190,7 @@
         mine = ((place >> 3) * 171) >> 9 == iota((2 * N_MP, 128), 0)
         parent.append(jnp.sum(jnp.where(mine, named, 0.0), axis=0, keepdims=True))
     parent = jnp.concatenate(parent, axis=1).astype(i32)
-    device = (parent >> 8) * 16 + ((parent >> 3) & 1) * 8 + ((parent >> 4) & 7)
-    line = device * 4 + ((parent >> 7) & 1) * 2 + (parent & 1)
+    line = (((parent >> 3) & 15) * 8 + (parent >> 8)) * 4 + ((parent >> 7) & 1) * 2 + (parent & 1)
     key = rows_of(line.astype(f32), N_DP * N_MP)
 
     weighted = (keep_ref[...] * scale).astype(bf16).astype(f32) * count_ref[0:1, :]
@@ -204,10 +203,7 @@
 
 
 def spread_kernel(in_ref, out_ref):
-    total = jnp.sum(in_ref[...].astype(f32).reshape(8, 8, 8, 128), axis=1)
-    total = total + pltpu.roll(total, 4, 1)
-    total = total.reshape(4, 2, 8, 128)
-    total = jnp.where(iota((4, 8, 128), 1) < 4, total[:, 0], total[:, 1])
+    total = jnp.sum(in_ref[...].astype(f32).reshape(N_DP // 2, 32, 128), axis=0).reshape(4, 8, 128)
     band, part = iota((2, 8, 128), 2) >> 5, iota((2, 8, 128), 1) >> 1
     even = jnp.concatenate([total[0:1], total[2:3]], axis=0)
     odd = jnp.concatenate([total[1:2], total[3:4]], axis=0)
@@ -319,7 +315,7 @@
         counts,
         spaces=(pltpu.VMEM, pltpu.VMEM),
     )
-    parts = exchange(partial.reshape(peers, 4, 128), ("y", "core", "z")).reshape(4 * peers, 128)
+    parts = exchange(partial.reshape(peers, 4, 128), ("z", "core", "y")).reshape(4 * peers, 128)
     parents = call(spread_kernel, shape((N_DP, 32, 128), bf16), parts)
     level3, level2 = call(
         finish_kernel,

time: 88.8 us -> 89 us (level)
  no operation moved by 1% of the time
where the time goes in v11:
time: 89 us; the launch traced here: 88.7 us
  blocking collectives  82.9 us (93%)
  Pallas kernels  5.17 us (6%)
    all_to_all x4, blocking collectives, exchange(): return lax.all_to_all(x, axis, 0, 0, tiled=True)  82.9 us
    pallas_call x5, Pallas kernels, call(): pl.pallas_call(kernel, out_shape=out, in_specs=[pl.BlockSpec(memory_space...  5.17 us

profile of v11, /device:TPU:1, one launch (start us, length us, event | category | flops | bytes accessed | tf_op | source)
XLA Modules:
  0.0 88.7 jit_solution(4341479234030993631)
XLA Ops:
  0.6 2.1 %shard_map.50 = bf16[1088,128]{1,0:T(8,128)(2,1)S(1)} custom-call(s32[1,2048]{1,0:T(1,128)} %bitcast.14, bf16[64,2048]{1,0:T(8,128)(2,1)} %bitcast.13), custom_call_target="tpu_custom_call" | custom-call | tf_op jit(solution)/shard_map/pallas_call | solution.py:264
  2.7 27.4 %all_to_all.20 = bf16[32,17,2,128]{3,2,1,0:T(2,128)(2,1)S(1)} all-to-all(bf16[32,17,2,128]{3,2,1,0:T(2,128)(2,1)S(1)} %bitcast.9), channel_id=1, replica_groups=mesh['z'=8,'xh'=2,'core'=2,'y'=8,'xl'=2] {'z','xh','core'}, dimensions={0} | all-to-all | bytes 557056 | tf_op jit(solution)/shard_map/all_to_all | solution.py:280
  30.2 1.4 %shard_map.51 = (bf16[32,16,128]{2,1,0:T(8,128)(2,1)S(1)}, f32[32,768]{1,0:T(8,128)S(1)}, f32[8,768]{1,0:T(8,128)S(1)}) custom-call(s32[1,24]{1,0:T(1,128)} %bitcast.15, bf16[1088,128]{1,0:T(8,128)(2,1)S(1)} %bitcast.8), custom_call_target="tpu_custom_call" | custom-call | tf_op jit(solution)/shard_map/pallas_call | solution.py:264
  31.6 17.3 %all_to_all.21.in_ref = bf16[32,16,128]{2,1,0:T(8,128)(2,1)S(1)} all-to-all(bf16[32,16,128]{2,1,0:T(8,128)(2,1)S(1)} %get-tuple-element.9), channel_id=1, replica_groups=mesh['z'=8,'xh'=2,'core'=2,'y'=8,'xl'=2] {'y','xh','xl'}, dimensions={0} | all-to-all | bytes 262144 | tf_op jit(solution)/shard_map/all_to_all | solution.py:280
  48.8 0.5 shard_map.52
  49.4 19.9 %all_to_all.22 = bf16[128,4,128]{2,1,0:T(4,128)(2,1)S(1)} all-to-all(bf16[128,4,128]{2,1,0:T(4,128)(2,1)S(1)} %bitcast.12), channel_id=1, replica_groups=mesh['z'=8,'xh'=2,'core'=2,'y'=8,'xl'=2] {'z','core','y'}, dimensions={0} | all-to-all | bytes 262144 | tf_op jit(solution)/shard_map/all_to_all | solution.py:280
  69.3 0.2 shard_map.53
  69.5 18.2 %all_to_all.23.in_ref = bf16[64,16,128]{2,1,0:T(8,128)(2,1)S(1)} all-to-all(bf16[64,16,128]{2,1,0:T(8,128)(2,1)S(1)} %bitcast.10), channel_id=1, replica_groups=mesh['z'=8,'xh'=2,'core'=2,'y'=8,'xl'=2] {'z','xh','core','xl'}, dimensions={0} | all-to-all | bytes 524288 | tf_op jit(solution)/shard_map/all_to_all | solution.py:280
  87.7 1.0 %shard_map.54 = (bf16[128,1024]{1,0:T(8,128)(2,1)}, bf16[24,1024]{1,0:T(8,128)(2,1)}) custom-call(bf16[64,16,128]{2,1,0:T(8,128)(2,1)S(1)} %all_to_all.23.in_ref, bf16[24,1024]{1,0:T(8,128)(2,1)S(1)} %get-tuple-element.13.level2_ref), custom_call_target="tpu_custom_call" | custom-call | tf_op jit(solution)/shard_map/pallas_call | solution.py:264
